TPU v7x, 512 devices: a whole 4x4x16 slice. The times are simulated.
512 devices in a mesh: dp: 64 (over y, x, z_hi, core), tensor: 8 (over z_lo).
Axes of the slice: x: 4, y: 4, z: 16 (z_hi: 2, z_lo: 8; z = z_hi * 8 + z_lo), core: 2. Of those that a mesh axis runs over, the one named last changes fastest.
Arguments:
- trainer_key_inputs: bfloat16 [131072, 4096], P('dp', 'tensor'), may hold values from -6 to 6
- cotangent: bfloat16 [131072, 512], P('dp', 'tensor'), may hold values from -6 to 6
- adapter_down_factor: float32 [4096, 64], P('tensor'), may hold values from -0.09375 to 0.09375
- adapter_up_factor: float32 [64, 512], P(None, 'tensor'), may hold values from -0.75 to 0.75
- frozen_key_weight: bfloat16 [4096, 512], P('tensor'), may hold values from -0.09375 to 0.09375
- hidden: bfloat16 [16384, 4, 4096], P('dp', None, 'tensor'), may hold values from -6 to 6
- positions: int32 [16384], P(('dp', 'tensor')), may hold values from 0 to 4091
- key_norm_gain: float32 [128], replicated, may hold values from 0.5 to 1.5
Outputs:
- keys: bfloat16 [16384, 4, 512], P(('dp', 'tensor'))
- updated_down_factor: float32 [4096, 64], P('tensor')
- updated_up_factor: float32 [64, 512], P(None, 'tensor')
All inputs are finite; a program needn't handle non-finite values.
Results may differ from a plain program's by a relative error of at most 0.009.
Values may be sent and summed in bfloat16 or wider, within the bound.
No kernel may reach another device: no remote copies, remote signals or barrier semaphores. Data moves between devices by JAX's collectives and lax.ppermute only.
A program may use at most 64 MiB of HBM per device.

v0:
```python
import jax
import jax.numpy as jnp
from jax import lax
from jax.sharding import PartitionSpec as P

HEAD_DIM = 128
KV_HEADS = 4
STEPS = 4


adapter_scale = 2.0
step_length = 8.0
epsilon = 1e-06
theta_base = 1000000.0


def rotate(normed, starts):
    half = HEAD_DIM // 2
    index = jnp.arange(half, dtype=jnp.float32)
    freqs = jnp.exp(-jnp.log(jnp.float32(theta_base)) * 2.0 * index / HEAD_DIM)
    places = (starts[:, None] + jnp.arange(STEPS, dtype=jnp.int32)[None, :]).astype(jnp.float32)
    angle = places[:, :, None, None] * freqs[None, None, None, :]
    cosine = jnp.cos(angle)
    sine = jnp.sin(angle)
    first = normed[..., :half]
    second = normed[..., half:]
    return jnp.concatenate(
        [first * cosine - second * sine, second * cosine + first * sine], axis=-1
    )


def reduce_over_rows(left, right):
    return lax.dot_general(
        left, right, (((0,), (0,)), ((), ())), preferred_element_type=jnp.float32
    )


def on_device(
    trainer_key_inputs,
    cotangent,
    adapter_down_factor,
    adapter_up_factor,
    frozen_key_weight,
    hidden,
    positions,
    key_norm_gain,
):
    down_factor_slice = adapter_down_factor.astype(jnp.bfloat16)
    up_factor_slice = adapter_up_factor.astype(jnp.bfloat16)
    down_part = jnp.dot(trainer_key_inputs, down_factor_slice, preferred_element_type=jnp.float32)
    back_part = lax.dot_general(
        cotangent, up_factor_slice, (((1,), (1,)), ((), ())), preferred_element_type=jnp.float32
    )
    down_sum, back_sum = lax.psum((down_part, back_part), "tensor")
    down_activation = down_sum.astype(jnp.bfloat16)
    backward_activation = back_sum.astype(jnp.bfloat16)
    down_gradient = adapter_scale * reduce_over_rows(trainer_key_inputs, backward_activation)
    up_gradient = adapter_scale * reduce_over_rows(down_activation, cotangent)
    down_gradient, up_gradient = lax.psum((down_gradient, up_gradient), "dp")
    total = lax.psum(
        jnp.sum(down_gradient * down_gradient) + jnp.sum(up_gradient * up_gradient), "tensor"
    )
    factor_matrix = step_length / jnp.sqrt(total + epsilon)
    updated_down_factor = adapter_down_factor - factor_matrix * down_gradient
    updated_up_factor = adapter_up_factor - factor_matrix * up_gradient
    a_new_low = updated_down_factor.astype(jnp.bfloat16)
    b_new_low = lax.all_gather(updated_up_factor.astype(jnp.bfloat16), "tensor", axis=1, tiled=True)
    rows_here = hidden.shape[0]
    flat = hidden.reshape(rows_here * STEPS, hidden.shape[2])
    own_rows = positions.shape[0]
    begin_row = lax.axis_index("tensor") * own_rows * STEPS
    rank_part = jnp.dot(flat, a_new_low, preferred_element_type=jnp.float32)
    base_part = jnp.dot(flat, frozen_key_weight, preferred_element_type=jnp.float32)
    rank_full = lax.psum(rank_part, "tensor")
    base_full = lax.psum(base_part.astype(jnp.bfloat16), "tensor").astype(jnp.float32)
    rank_activation = lax.dynamic_slice_in_dim(rank_full, begin_row, own_rows * STEPS, 0)
    frozen_output = lax.dynamic_slice_in_dim(base_full, begin_row, own_rows * STEPS, 0)
    up_factor_expanded = b_new_low.astype(jnp.float32)
    key_projection = frozen_output + adapter_scale * jnp.dot(
        rank_activation,
        up_factor_expanded,
        precision=lax.Precision.HIGHEST,
        preferred_element_type=jnp.float32,
    )
    heads = key_projection.reshape(own_rows, STEPS, KV_HEADS, HEAD_DIM)
    normed = (
        heads * lax.rsqrt(jnp.mean(heads * heads, axis=-1, keepdims=True) + epsilon) * key_norm_gain
    )
    keys = (
        rotate(normed, positions).reshape(own_rows, STEPS, KV_HEADS * HEAD_DIM).astype(jnp.bfloat16)
    )
    return (keys, updated_down_factor, updated_up_factor)


def solution(mesh):
    in_specs = (
        P("dp", "tensor"),
        P("dp", "tensor"),
        P("tensor", None),
        P(None, "tensor"),
        P("tensor", None),
        P("dp", None, "tensor"),
        P(("dp", "tensor")),
        P(),
    )
    out_specs = (P(("dp", "tensor"), None, None), P("tensor", None), P(None, "tensor"))
    return jax.shard_map(
        on_device, mesh=mesh, in_specs=in_specs, out_specs=out_specs, check_vma=False
    )
```

profile of v0, /device:TPU:6, one launch (start us, length us, event | category | flops | bytes accessed | tf_op | source)
XLA Modules:
  0.0 1421.8 jit_solution(6101504956448460435)
XLA Ops:
  7.2 0.0 copy-start
  7.2 0.0 copy-start.8
  7.2 0.0 copy-start.1
  7.2 0.0 all-reduce.8.cloned.1.call-start
  7.2 1.5 copy-done
  8.8 1.6 fusion.5
  10.4 0.0 copy-done.8
  10.4 0.0 copy-done.1
  10.4 0.2 fusion.8
  10.6 114.3 %all-reduce.11 = (bf16[2048,64]{0,1:T(8,128)(2,1)}, bf16[2048,64]{0,1:T(8,128)(2,1)}) all-reduce(f32[2048,64]{0,1:T(8,128)S(1)} %fusion.5, f32[2048,64]{0,1:T(8,128)S(1)} %fusion.8), channel_id=1, replica_groups=mesh['dp'=64,'tensor'=8] {'tensor'}, use_global_device_ids=true, to_apply=%region_4.0 | all-reduce | flops 262144 | bytes 1572864 | tf_op jit(solution)/shard_map/psum | solution.py:54
  124.9 0.0 copy-start.7
  124.9 2.1 fusion.1
  127.0 0.0 copy-start.4
  127.0 0.0 all-reduce.8.cloned.1.call-update
  127.1 0.0 all-reduce.10.cloned.1.call-start
  127.1 0.0 copy-done.7
  127.1 0.2 convolution_multiply_fusion.2
  127.3 496.8 %psum.53 = f32[64,64]{1,0:T(8,128)S(1)} all-reduce(f32[64,64]{1,0:T(8,128)S(1)} %convolution_multiply_fusion.2), channel_id=1, replica_groups=mesh['dp'=64,'tensor'=8] {'dp'}, use_global_device_ids=true, to_apply=%region_5.0 | all-reduce | flops 4096 | bytes 32768 | tf_op jit(solution)/shard_map/psum | solution.py:59
  624.2 0.0 copy-start.5
  624.2 0.6 multiply_reduce_fusion.2
  624.8 478.5 %all-reduce.8.cloned.1.call-done = f32[512,64]{0,1:T(8,128)} async-done(((f32[512,64]{0,1:T(8,128)}), f32[512,64]{0,1:T(8,128)}) %all-reduce.8.cloned.1.call-update) | async-done | bytes 131088 | tf_op jit(solution)/shard_map/psum | solution.py:59
  1103.2 0.0 copy-start.2
  1103.2 1.6 multiply_reduce_fusion.1
  1104.9 0.0 copy-done.5
  1106.2 1.3 reshape.60
  1107.5 33.3 %psum.54 = f32[]{:T(128)} all-reduce(f32[]{:T(128)S(6)} %add.59), channel_id=1, replica_groups=mesh['dp'=64,'tensor'=8] {'tensor'}, use_global_device_ids=true, to_apply=%region_7.0 | all-reduce | flops 1 | bytes 8 | tf_op jit(solution)/shard_map/psum | solution.py:60
  1141.5 0.0 copy-done.4
  1141.5 0.0 copy-done.2
  1141.5 0.0 copy-start.3
  1141.5 1.1 convolution_bitcast_fusion
  1142.7 0.0 copy-start.10
  1142.7 0.0 all-reduce.10.cloned.1.call-update
  1142.7 0.0 copy-start.6
  1142.7 0.0 copy-start.9
  1142.7 0.0 all-reduce.6.cloned.1.call-start
  1142.8 2.8 convolution_convert_fusion
  1145.6 0.0 copy-done.3
  1145.6 0.0 copy-start.11
  1145.6 0.0 all-reduce.6.cloned.1.call-update
  1145.6 0.0 copy-done.10
  1145.6 0.1 add_convert_fusion.1
  1145.7 0.5 multiply_cosine_fusion
  1146.2 0.0 copy-done.6
  1146.2 0.0 copy-done.9
  1146.2 0.6 fusion.11
  1146.9 0.1 copy.14
  1147.0 46.5 %all_gather.3 = bf16[64,512]{0,1:T(8,128)(2,1)S(1)} all-gather(bf16[64,64]{0,1:T(8,128)(2,1)S(1)} %copy.14), channel_id=1, replica_groups=mesh['dp'=64,'tensor'=8] {'tensor'}, dimensions={1}, use_global_device_ids=true | all-gather | bytes 73728 | tf_op jit(solution)/shard_map/all_gather | solution.py:67
  1193.4 93.7 %all-reduce.10.cloned.1.call-done = f32[1024,64]{0,1:T(8,128)} async-done(((f32[1024,64]{0,1:T(8,128)}), f32[1024,64]{0,1:T(8,128)}) %all-reduce.10.cloned.1.call-update) | async-done | bytes 262160 | tf_op jit(solution)/shard_map/psum | solution.py:74
  1287.1 124.9 %all-reduce.6.cloned.1.call-done = bf16[1024,512]{1,0:T(8,128)(2,1)} async-done(((bf16[1024,512]{1,0:T(8,128)(2,1)}), bf16[1024,512]{1,0:T(8,128)(2,1)}) %all-reduce.6.cloned.1.call-update) | async-done | bytes 1048592 | tf_op jit(solution)/shard_map/psum | solution.py:75
  1412.0 1.3 fusion
  1413.3 0.1 reshape.61
  1413.4 0.3 multiply_reduce_fusion
  1413.6 0.1 copy.15
  1413.8 0.1 copy.16
  1413.9 0.0 copy-done.11
  1413.9 0.2 multiply_multiply_fusion
  1414.1 0.3 subtract_convert_fusion
  1414.4 0.2 pad_maximum_fusion
  1414.6 0.7 convert_element_type.45
  (3 shorter events, 0.0 us)
Async XLA Ops:
  7.2 1.6 copy-start
  7.2 3.2 copy-start.8
  7.2 3.2 copy-start.1
  7.2 1096.0 %all-reduce.8.cloned.1.call-start = ((), (), s32[]{:S(2)}) async-start(), calls=%async_computation.1 | async-start | bytes 262144 | tf_op jit(solution)/shard_map/psum | solution.py:59
  124.9 2.2 copy-start.7
  127.0 1014.4 %copy-start.4 = (f32[512,64]{0,1:T(8,128)S(1)}, f32[512,64]{0,1:T(8,128)}, u32[]{:S(2)}) copy-start(f32[512,64]{0,1:T(8,128)} %param.10) | copy-start | bytes 393220
  127.1 1160.1 %all-reduce.10.cloned.1.call-start = ((), (), s32[]{:S(2)}) async-start(), calls=%async_computation.2 | async-start | bytes 524288 | tf_op jit(solution)/shard_map/psum | solution.py:74
  624.2 480.7 %copy-start.5 = (f32[64,64]{1,0:T(8,128)}, f32[64,64]{1,0:T(8,128)S(1)}, u32[]{:S(2)}) copy-start(f32[64,64]{1,0:T(8,128)S(1)} %psum.53) | copy-start | bytes 49156
  1103.2 38.2 %copy-start.2 = (f32[512,64]{0,1:T(8,128)S(1)}, f32[512,64]{0,1:T(8,128)}, u32[]{:S(2)}) copy-start(f32[512,64]{0,1:T(8,128)} %all-reduce.8.cloned.1.call-done) | copy-start | bytes 393220
  1141.5 4.0 copy-start.3
  1142.7 2.9 copy-start.10
  1142.7 3.5 copy-start.6
  1142.7 3.5 copy-start.9
  1142.7 269.3 %all-reduce.6.cloned.1.call-start = ((), (), s32[]{:S(2)}) async-start(), calls=%async_computation | async-start | bytes 2097152 | tf_op jit(solution)/shard_map/psum | solution.py:75
  1145.6 268.3 %copy-start.11 = (f32[128]{0:T(128)S(1)}, f32[128]{0:T(128)}, u32[]{:S(2)}) copy-start(f32[128]{0:T(128)} %param.15) | copy-start | bytes 1540
Sparse Core Ops, SparseCore 0:
  127.2 976.0 all-reduce.7
  1142.8 144.2 all-reduce.9
  1290.1 121.9 all-reduce.5
where the time goes:
time: 1420 us
  waiting for transfers between devices  697 us (49%)
  blocking collectives  691 us (49%)
  between operations  16 us (1%)
    psum x1, blocking collectives, on_device(): down_gradient, up_gradient = lax.psum((down_gradient, up_gradient), 'dp')  497 us
    psum x1, waiting for transfers between devices, on_device(): down_gradient, up_gradient = lax.psum((down_gradient, up_gradient), 'dp')  478 us
    psum x1, waiting for transfers between devices, on_device(): lax.psum(base_part.astype(jnp.bfloat16), 'tensor').astype(jnp.float32)  125 us
    psum x1, blocking collectives, on_device(): down_sum, back_sum = lax.psum((down_part, back_part), 'tensor')  114 us
    psum x1, waiting for transfers between devices, on_device(): rank_full = lax.psum(rank_part, 'tensor')  93.7 us
    all_gather x1, blocking collectives, on_device(): lax.all_gather(updated_up_factor.astype(jnp.bfloat16), 'tensor', axis=1,...  46.5 us
    psum x1, blocking collectives, on_device(): lax.psum(jnp.sum(down_gradient * down_gradient) + jnp.sum(up_gradient * u...  33.3 us
  transfers between devices with their start and end apart: 3, of which 3 were waited for; matrix products, arithmetic and copies ran while one was open for 0% of the time, Pallas kernels for 0%

commit v1 on v0

v1 whole, which is shorter than its diff:
```python
import jax
import jax.numpy as jnp
from jax import lax
from jax.sharding import Mesh
from jax.sharding import PartitionSpec as P

HEAD_DIM = 128
KV_HEADS = 4
STEPS = 4

adapter_scale = 2.0
step_length = 8.0
epsilon = 1e-06
theta_base = 1000000.0

TENSOR = ("t2", "t1", "t0")
PLANE = ("y", "x", "core")
SWAP = [(0, 1), (1, 0)]
bf16 = jnp.bfloat16
f32 = jnp.float32


def rotate(normed, starts):
    half = HEAD_DIM // 2
    index = jnp.arange(half, dtype=jnp.float32)
    freqs = jnp.exp(-jnp.log(jnp.float32(theta_base)) * 2.0 * index / HEAD_DIM)
    places = (starts[:, None] + jnp.arange(STEPS, dtype=jnp.int32)[None, :]).astype(jnp.float32)
    angle = places[:, :, None, None] * freqs[None, None, None, :]
    cosine = jnp.cos(angle)
    sine = jnp.sin(angle)
    first = normed[..., :half]
    second = normed[..., half:]
    return jnp.concatenate(
        [first * cosine - second * sine, second * cosine + first * sine], axis=-1
    )


def dot(left, right, dims):
    return lax.dot_general(left, right, (dims, ((), ())), preferred_element_type=f32)


def fold(rows):
    n = rows.shape[-2] // 2
    return jnp.concatenate([rows[..., :n, :], rows[..., n:, :]], axis=-1)


def unfold(rows):
    return jnp.concatenate([rows[..., :64], rows[..., 64:]], axis=-2)


def on_device(x, c, a, b, w, hidden, positions, gain):
    a_low = a.astype(bf16)
    b_low = b.astype(bf16)

    down_part = dot(x, a_low, ((1,), (0,))).astype(bf16)
    rows = jnp.concatenate([c, down_part], axis=1).reshape(8, 256, 128)
    send = jnp.concatenate([rows, jnp.broadcast_to(fold(b_low), (8, 32, 128))], axis=1)
    got = lax.all_to_all(send, TENSOR, 0, 0)
    c_rows = got[:, :256, :64]
    b_full = unfold(got[:, 256:])
    down = got[:, :256, 64:].astype(f32).sum(axis=0).astype(bf16)
    back = jnp.einsum("jtc,jkc->tk", c_rows, b_full, preferred_element_type=f32).astype(bf16)
    up_part = jnp.einsum("tk,jtc->jkc", down, c_rows, preferred_element_type=f32).astype(bf16)

    send = jnp.concatenate([jnp.broadcast_to(fold(back), (8, 128, 128)), fold(up_part)], axis=1)
    got = lax.all_to_all(send, TENSOR, 0, 0)
    back_all = unfold(got[:, :128]).reshape(2048, 64)
    up_part = got[:, 128:].astype(f32).sum(axis=0)
    down_part = dot(back_all, x, ((0,), (0,)))

    flat = hidden.reshape(4, 2, 128, 512)
    i0, i1, i2 = (lax.axis_index(n) for n in ("t0", "t1", "t2"))
    weight = jnp.concatenate([w, a_low, jnp.zeros_like(a_low)], axis=1)

    def project(which):
        part = lax.dynamic_index_in_dim(flat, which, 1, keepdims=False).reshape(512, 512)
        return dot(part, weight, ((1,), (0,))).astype(bf16)

    sent = project(1 - i0).reshape(2, 2, 128, 640)
    kept = project(i0).reshape(2, 2, 128, 640)

    tiles = down_part.reshape(8, 8, 4, 128).transpose(0, 2, 1, 3).reshape(32, 8, 128)
    send = jnp.concatenate(
        [tiles, up_part[:, None, :], jnp.zeros((32, 7, 128), f32)], axis=1
    ).astype(bf16)
    send, sent, kept = lax.optimization_barrier((send, sent, kept))
    came = lax.ppermute(sent, "t0", SWAP)
    got = lax.all_to_all(send, PLANE, 0, 0)
    mine = got.astype(f32).sum(axis=0).astype(bf16)
    mine, came = lax.optimization_barrier((mine, came))

    kept = kept + came
    sent = lax.dynamic_index_in_dim(kept, 1 - i1, 1, keepdims=False)
    kept = lax.dynamic_index_in_dim(kept, i1, 1, keepdims=False)
    mine, sent, kept = lax.optimization_barrier((mine, sent, kept))
    came = lax.ppermute(sent, "t1", SWAP)
    other = lax.ppermute(mine, "zh", SWAP)
    mine = (mine.astype(f32) + other.astype(f32)).astype(bf16)
    mine, came = lax.optimization_barrier((mine, came))

    kept = kept + came
    sent = lax.dynamic_index_in_dim(kept, 1 - i2, 0, keepdims=False)
    kept = lax.dynamic_index_in_dim(kept, i2, 0, keepdims=False)
    send = jnp.broadcast_to(mine, (32, 16, 128))
    send, sent, kept = lax.optimization_barrier((send, sent, kept))
    came = lax.ppermute(sent, "t2", SWAP)
    got = lax.all_to_all(send, PLANE, 0, 0)
    got, came = lax.optimization_barrier((got, came))
    kept = kept.astype(f32) + came.astype(f32)

    tiles = got[:, :8].reshape(8, 4, 8, 128).transpose(0, 2, 1, 3).reshape(64, 512)
    up_low = got[:, 8]
    down_grad = adapter_scale * tiles.T.astype(f32)
    up_grad = adapter_scale * unfold(up_low.astype(f32))
    square = jnp.sum(down_grad * down_grad) + jnp.sum(up_grad * up_grad)
    high = square.astype(bf16)
    low = (square - high.astype(f32)).astype(bf16)
    rank_part = dot(hidden.reshape(1024, 512), tiles, ((1,), (1,))).astype(bf16)
    scalars = jnp.concatenate([jnp.full((8, 8, 128), high), jnp.full((8, 8, 128), low)], axis=1)
    send = jnp.concatenate(
        [fold(rank_part.reshape(8, 128, 64)), jnp.broadcast_to(up_low, (8, 32, 128)), scalars],
        axis=1,
    )
    got = lax.all_to_all(send, TENSOR, 0, 0)
    total = jnp.sum(got[:, 96, 0].astype(f32) + got[:, 104, 0].astype(f32))
    factor = step_length / jnp.sqrt(total + epsilon)
    updated_down = a - factor * down_grad
    updated_up = b - factor * up_grad

    rank_new = unfold(got[:, :64].astype(f32).sum(axis=0)) * adapter_scale
    base = kept[:, :512]
    rank_act = kept[:, 512:576] - factor * rank_new
    return base, rank_act, b_full, got[:, 64:96], factor, updated_down, updated_up, positions, gain


def finish(base, rank_act, b_full, up_all, factor, updated_down, updated_up, positions, gain):
    up_new = (b_full.astype(f32) - factor * adapter_scale * unfold(up_all).astype(f32)).astype(bf16)
    up_new = up_new.transpose(1, 0, 2).reshape(64, 512)
    proj = base + adapter_scale * jnp.dot(
        rank_act, up_new.astype(f32), precision=lax.Precision.HIGHEST, preferred_element_type=f32
    )
    own = positions.shape[0]
    heads = proj.reshape(own, STEPS, KV_HEADS, HEAD_DIM)
    normed = heads * lax.rsqrt(jnp.mean(heads * heads, axis=-1, keepdims=True) + epsilon) * gain
    keys = rotate(normed, positions).reshape(own, STEPS, KV_HEADS * HEAD_DIM).astype(bf16)
    return keys, updated_down, updated_up


def whole(*args):
    return finish(*on_device(*args))


def solution(mesh):
    names = ("y", "x", "zh", "core") + TENSOR
    fine = Mesh(mesh.devices.reshape(4, 4, 2, 2, 2, 2, 2), names)
    dp = ("y", "x", "zh", "core")
    in_specs = (
        P(dp, TENSOR),
        P(dp, TENSOR),
        P(TENSOR, None),
        P(None, TENSOR),
        P(TENSOR, None),
        P(dp, None, TENSOR),
        P(dp + TENSOR),
        P(),
    )
    out_specs = (P(dp + TENSOR, None, None), P(TENSOR, None), P(None, TENSOR))
    return jax.shard_map(whole, mesh=fine, in_specs=in_specs, out_specs=out_specs, check_vma=False)
```

time: 1420 us -> 170 us (0.12)
  blocking collectives: 691 us -> 43.9 us
  waiting for transfers between devices: 697 us -> 51.4 us
  starting transfers between devices: 0.12 us -> 40.6 us
    psum x3 -> x0, waiting for transfers between devices: 697 us -> none  [the longest x1 478 us: on_device(): down_gradient, up_gradient = lax.psum((down_gradient, up_gradient), 'dp')]
    psum x3 -> x0, blocking collectives: 644 us -> none  [the longest x1 497 us: on_device(): down_gradient, up_gradient = lax.psum((down_gradient, up_gradient), 'dp')]
    all_gather x1 -> x0, blocking collectives: 46.5 us -> none  [on_device(): lax.all_gather(updated_up_factor.astype(jnp.bfloat16), 'tensor', axis=1,...]
    all_to_all x0 -> x1, blocking collectives: none -> 43.9 us  [on_device(): got = lax.all_to_all(send, TENSOR, 0, 0)]
    all_to_all x0 -> x4, waiting for transfers between devices: none -> 38.4 us  [the longest x2 26.5 us: on_device(): got = lax.all_to_all(send, TENSOR, 0, 0)]
    all_to_all x0 -> x4, starting transfers between devices: none -> 23.5 us  [the longest x2 14.9 us: on_device(): got = lax.all_to_all(send, PLANE, 0, 0)]
    ppermute x0 -> x4, starting transfers between devices: none -> 17.1 us  [the longest x1 8.22 us: on_device(): other = lax.ppermute(mine, 'zh', SWAP)]
  transfers between devices with their start and end apart: 3 -> 8, of which waited for: 3 -> 7; matrix products, arithmetic and copies ran while one was open for 0% -> 4% of each run, Pallas kernels for 0% -> 0%
where the time goes in v1:
time: 170 us; the launch traced here: 168 us
  waiting for transfers between devices  51.4 us (30%)
  blocking collectives  43.9 us (26%)
  starting transfers between devices  40.6 us (24%)
  local copies, waits for them, and re-layouts  11.2 us (7%)
  other arithmetic  9.9 us (6%)
  matrix products  8.17 us (5%)
  between operations  3.2 us (2%)
    all_to_all x1, blocking collectives, on_device(): got = lax.all_to_all(send, TENSOR, 0, 0)  43.9 us
    all_to_all x2, waiting for transfers between devices, on_device(): got = lax.all_to_all(send, TENSOR, 0, 0)  26.5 us
    all_to_all x2, starting transfers between devices, on_device(): got = lax.all_to_all(send, PLANE, 0, 0)  14.9 us
    all_to_all x2, waiting for transfers between devices, on_device(): got = lax.all_to_all(send, PLANE, 0, 0)  11.9 us
    all_to_all x2, starting transfers between devices, on_device(): got = lax.all_to_all(send, TENSOR, 0, 0)  8.61 us
    ppermute x1, starting transfers between devices, on_device(): other = lax.ppermute(mine, 'zh', SWAP)  8.22 us
    dot_general x5, matrix products, dot(): lax.dot_general(left, right, (dims, ((), ())), preferred_element_type=f32)  7.39 us
    ppermute x1, waiting for transfers between devices, on_device(): other = lax.ppermute(mine, 'zh', SWAP)  6.32 us
  transfers between devices with their start and end apart: 8, of which 7 were waited for; matrix products, arithmetic and copies ran while one was open for 4% of the time, Pallas kernels for 0%

profile of v1, /device:TPU:6, one launch (start us, length us, event | category | flops | bytes accessed | tf_op | source)
XLA Modules:
  0.0 168.2 jit_solution(3572240574908200418)
XLA Ops:
  0.6 1.1 copy.71
  1.7 2.4 %convolution_convert_fusion = bf16[2048,64]{0,1:T(8,128)(2,1)S(1)} fusion(bf16[2048,512]{1,0:T(8,128)(2,1)} %param.8, bf16[512,64]{1,0:T(8,128)(2,1)S(1)} %copy.71), kind=kOutput, calls=%fused_computation | convolution fusion | flops 134348800 | bytes 2424832 | tf_op jit(solution)/shard_map/dot_general | solution.py:39
  4.2 0.3 copy.91
  4.5 0.4 copy-done.9
  4.9 0.1 pad_maximum_fusion.8
  5.0 43.9 %all_to_all.25 = bf16[8,288,128]{2,1,0:T(8,128)(2,1)S(1)} all-to-all(bf16[8,288,128]{2,1,0:T(8,128)(2,1)S(1)} %pad_maximum_fusion), channel_id=1, replica_groups=mesh['y'=4,'x'=4,'zh'=2,'core'=2,'t2'=2,'t1'=2,'t0'=2] {'t2','t1','t0'}, dimensions={0} | all-to-all | bytes 1179648 | tf_op jit(solution)/shard_map/all_to_all | solution.py:58
  48.9 0.1 fusion.25
  49.0 0.3 fusion.3
  49.3 0.1 copy.74
  49.4 0.2 slice_reduce_fusion
  49.7 0.2 fusion.1
  50.0 0.8 maximum_maximum_fusion.3
  50.8 4.3 %all-to-all-start.1 = ((bf16[8,160,128]{2,1,0:T(8,128)(2,1)}), bf16[8,160,128]{2,1,0:T(8,128)(2,1)S(1)}, u32[]{:S(2)}, u32[]{:S(2)}) async-start(bf16[8,160,128]{2,1,0:T(8,128)(2,1)} %maximum_maximum_fusion.3), calls=%async_computation.1 | async-start | bytes 655360 | tf_op jit(solution)/shard_map/all_to_all | solution.py:66
  55.1 2.5 %copy.93 = bf16[512,2048]{1,0:T(8,128)(2,1)} copy(bf16[512,2048]{0,1:T(8,128)(2,1)S(1)} %bitcast.66) | data formatting | bytes 4194304 | tf_op jit(solution)/shard_map/dot_general | solution.py:39
  57.6 0.3 reshape.108
  58.2 0.6 copy-done.5
  58.8 0.2 copy-done.13
  59.0 1.4 convolution_convert_fusion.2
  60.4 1.4 convolution_convert_fusion.1
  61.9 12.2 %all-to-all-done.1 = bf16[8,160,128]{2,1,0:T(8,128)(2,1)S(1)} async-done(((bf16[8,160,128]{2,1,0:T(8,128)(2,1)}), bf16[8,160,128]{2,1,0:T(8,128)(2,1)S(1)}, u32[]{:S(2)}, u32[]{:S(2)}) %all-to-all-start.1) | async-done | bytes 327712 | tf_op jit(solution)/shard_map/all_to_all | solution.py:66
  74.0 0.1 fusion.26
  74.2 0.9 pad_maximum_fusion.2
  75.1 1.9 %copy.77 = bf16[2048,64]{0,1:T(8,128)(2,1)} copy(bf16[2048,64]{1,0:T(8,128)(2,1)} %bitcast.69) | data formatting | bytes 524288 | tf_op jit(solution)/shard_map/reshape | solution.py:67
  77.0 0.1 copy.96
  77.1 0.1 copy.81
  77.3 1.7 %convolution_convert_fusion.5 = bf16[8,8,4,128]{3,1,2,0:T(8,128)(2,1)S(1)} fusion(bf16[4,128,2048,1]{2,1,0,3:T(8,128)(2,1)S(1)} %bitcast.67, bf16[2048,64]{0,1:T(8,128)(2,1)} %copy.77), kind=kOutput, calls=%fused_computation.9 | convolution fusion | flops 134250496 | bytes 2424832 | tf_op jit(solution)/shard_map/dot_general | solution.py:39
  79.0 0.8 maximum_maximum_fusion.5
  79.7 3.8 %collective-permute-start = (bf16[2,2,128,640]{3,2,1,0:T(8,128)(2,1)}, bf16[2,2,128,640]{3,2,1,0:T(8,128)(2,1)S(1)}, u32[]{:S(2)}, u32[]{:S(2)}) collective-permute-start(bf16[2,2,128,640]{3,2,1,0:T(8,128)(2,1)} %bitcast.16), channel_id=1, source_target_pairs={{0,1},{1,0},{2,3},{3,2},{4,5},{5,4},{6,7},{7,6},{8,9},{9,8},{10,11... | collective-permute-start | bytes 1966088 | tf_op jit(solution)/shard_map/ppermute | solution.py:87
  83.5 7.6 %all-to-all-start.2 = ((bf16[32,16,128]{2,1,0:T(8,128)(2,1)}), bf16[32,16,128]{2,1,0:T(8,128)(2,1)S(1)}, u32[]{:S(2)}, u32[]{:S(2)}) async-start(bf16[32,16,128]{2,1,0:T(8,128)(2,1)} %maximum_maximum_fusion.5), calls=%async_computation.2 | async-start | bytes 262144 | tf_op jit(solution)/shard_map/all_to_all | solution.py:88
  91.1 6.1 %all-to-all-done.2 = bf16[32,16,128]{2,1,0:T(8,128)(2,1)S(1)} async-done(((bf16[32,16,128]{2,1,0:T(8,128)(2,1)}), bf16[32,16,128]{2,1,0:T(8,128)(2,1)S(1)}, u32[]{:S(2)}, u32[]{:S(2)}) %all-to-all-start.2) | async-done | bytes 131104 | tf_op jit(solution)/shard_map/all_to_all | solution.py:88
  97.2 1.2 add.82
  98.5 1.9 %collective-permute-start.2 = (bf16[2,128,640]{2,1,0:T(8,128)(2,1)S(1)}, bf16[2,128,640]{2,1,0:T(8,128)(2,1)S(1)}, u32[]{:S(2)}, u32[]{:S(2)}) collective-permute-start(bf16[2,128,640]{2,1,0:T(8,128)(2,1)S(1)} %get-tuple-element.24), channel_id=1, source_target_pairs={{0,2},{2,0},{1,3},{3,1},{4,6},{6,4},{5,7},{7,5},{8,10},{10,8},{9,1... | collective-permute-start | bytes 983048 | tf_op jit(solution)/shard_map/ppermute | solution.py:96
  100.5 8.2 %collective-permute-start.1 = (bf16[16,128]{1,0:T(8,128)(2,1)S(1)}, bf16[16,128]{1,0:T(8,128)(2,1)S(1)}, u32[]{:S(2)}, u32[]{:S(2)}) collective-permute-start(bf16[16,128]{1,0:T(8,128)(2,1)S(1)} %reduce_sum.80), channel_id=1, source_target_pairs={{0,16},{16,0},{1,17},{17,1},{2,18},{18,2},{3,19},{19,3},{4,20},{20... | collective-permute-start | bytes 12296 | tf_op jit(solution)/shard_map/ppermute | solution.py:97
  108.7 6.3 %collective-permute-done.1 = bf16[16,128]{1,0:T(8,128)(2,1)S(1)} collective-permute-done((bf16[16,128]{1,0:T(8,128)(2,1)S(1)}, bf16[16,128]{1,0:T(8,128)(2,1)S(1)}, u32[]{:S(2)}, u32[]{:S(2)}) %collective-permute-start.1) | collective-permute-done | bytes 4128 | tf_op jit(solution)/shard_map/ppermute | solution.py:97
  115.0 3.0 %collective-permute-done.2 = bf16[2,128,640]{2,1,0:T(8,128)(2,1)S(1)} collective-permute-done((bf16[2,128,640]{2,1,0:T(8,128)(2,1)S(1)}, bf16[2,128,640]{2,1,0:T(8,128)(2,1)S(1)}, u32[]{:S(2)}, u32[]{:S(2)}) %collective-permute-start.2) | collective-permute-done | bytes 327712 | tf_op jit(solution)/shard_map/ppermute | solution.py:96
  118.2 0.7 broadcast_in_dim.39
  118.8 3.2 %collective-permute-start.3 = (bf16[128,640]{1,0:T(8,128)(2,1)S(1)}, bf16[128,640]{1,0:T(8,128)(2,1)S(1)}, u32[]{:S(2)}, u32[]{:S(2)}) collective-permute-start(bf16[128,640]{1,0:T(8,128)(2,1)S(1)} %get-tuple-element.30), channel_id=1, source_target_pairs={{0,4},{4,0},{1,5},{5,1},{2,6},{6,2},{3,7},{7,3},{8,12},{12,8},{9,1... | collective-permute-start | bytes 491528 | tf_op jit(solution)/shard_map/ppermute | solution.py:106
  122.0 7.3 %all-to-all-start.3 = ((bf16[32,16,128]{2,1,0:T(8,128)(2,1)}), bf16[32,16,128]{2,1,0:T(8,128)(2,1)S(1)}, u32[]{:S(2)}, u32[]{:S(2)}) async-start(bf16[32,16,128]{2,1,0:T(8,128)(2,1)} %broadcast_in_dim.39), calls=%async_computation.3 | async-start | bytes 262144 | tf_op jit(solution)/shard_map/all_to_all | solution.py:107
  129.3 0.3 reshape.115
  129.6 5.8 %all-to-all-done.3 = bf16[32,16,128]{2,1,0:T(8,128)(2,1)S(1)} async-done(((bf16[32,16,128]{2,1,0:T(8,128)(2,1)}), bf16[32,16,128]{2,1,0:T(8,128)(2,1)S(1)}, u32[]{:S(2)}, u32[]{:S(2)}) %all-to-all-start.3) | async-done | bytes 131104 | tf_op jit(solution)/shard_map/all_to_all | solution.py:107
  135.4 3.7 %collective-permute-done.3 = bf16[128,640]{1,0:T(8,128)(2,1)S(1)} collective-permute-done((bf16[128,640]{1,0:T(8,128)(2,1)S(1)}, bf16[128,640]{1,0:T(8,128)(2,1)S(1)}, u32[]{:S(2)}, u32[]{:S(2)}) %collective-permute-start.3) | collective-permute-done | bytes 163872 | tf_op jit(solution)/shard_map/ppermute | solution.py:106
  139.2 0.6 fusion.10
  139.8 0.6 multiply_reduce_fusion.1
  141.9 0.4 fusion.2
  142.4 0.2 copy.82
  142.6 0.8 maximum_maximum_fusion.4
  143.5 4.3 %all-to-all-start.4 = ((bf16[8,112,128]{2,1,0:T(8,128)(2,1)}), bf16[8,112,128]{2,1,0:T(8,128)(2,1)S(1)}, u32[]{:S(2)}, u32[]{:S(2)}) async-start(bf16[8,112,128]{2,1,0:T(8,128)(2,1)} %maximum_maximum_fusion.4), calls=%async_computation.4 | async-start | bytes 458752 | tf_op jit(solution)/shard_map/all_to_all | solution.py:124
  147.9 0.5 multiply_cosine_fusion
  148.4 14.4 %all-to-all-done.4 = bf16[8,112,128]{2,1,0:T(8,128)(2,1)S(1)} async-done(((bf16[8,112,128]{2,1,0:T(8,128)(2,1)}), bf16[8,112,128]{2,1,0:T(8,128)(2,1)S(1)}, u32[]{:S(2)}, u32[]{:S(2)}) %all-to-all-start.4) | async-done | bytes 229408 | tf_op jit(solution)/shard_map/all_to_all | solution.py:124
  162.8 0.6 fusion.19
  164.1 0.6 multiply_subtract_fusion
  164.7 0.7 fusion.12
  165.4 0.1 fusion.28
  165.6 0.1 copy.84
  165.7 0.1 reshape.117
  165.9 0.3 fusion
  166.2 0.1 reshape.118
  166.3 0.3 multiply_reduce_fusion
  166.6 0.1 copy.85
  166.7 0.1 copy.86
  166.8 0.2 multiply_multiply_fusion
  167.0 0.3 subtract_convert_fusion
  167.3 0.2 pad_maximum_fusion.4
  167.5 0.7 convert_element_type.129
  (63 shorter events, 1.3 us)
Async XLA Ops:
  0.6 3.5 %copy-start.6 = (bf16[2048,64]{0,1:T(8,128)(2,1)S(1)}, bf16[2048,64]{0,1:T(8,128)(2,1)}, u32[]{:S(2)}) copy-start(bf16[2048,64]{0,1:T(8,128)(2,1)} %param.9) | copy-start | bytes 786436
  1.7 2.4 %copy-start.4 = (bf16[512,64]{1,0:T(8,128)(2,1)}, bf16[512,64]{1,0:T(8,128)(2,1)S(1)}, u32[]{:S(2)}) copy-start(bf16[512,64]{1,0:T(8,128)(2,1)S(1)} %copy.71) | copy-start | bytes 196612
  4.1 0.8 copy-start.9
  49.0 1.0 copy-start.7
  49.7 5.4 %copy-start = (bf16[2048,512]{1,0:T(8,128)(2,1)S(1)}, bf16[2048,512]{1,0:T(8,128)(2,1)}, u32[]{:S(2)}) copy-start(bf16[2048,512]{1,0:T(8,128)(2,1)} %param.8) | copy-start | bytes 6291460
  50.8 23.2 %all-to-all-start.1 = ((bf16[8,160,128]{2,1,0:T(8,128)(2,1)}), bf16[8,160,128]{2,1,0:T(8,128)(2,1)S(1)}, u32[]{:S(2)}, u32[]{:S(2)}) async-start(bf16[8,160,128]{2,1,0:T(8,128)(2,1)} %maximum_maximum_fusion.3), calls=%async_computation.1 | async-start | bytes 655360 | tf_op jit(solution)/shard_map/all_to_all | solution.py:66
  55.1 2.5 %copy-start.2 = (bf16[256,4,512]{2,1,0:T(4,128)(2,1)S(1)}, bf16[256,4,512]{2,1,0:T(4,128)(2,1)}, u32[]{:S(2)}) copy-start(bf16[256,4,512]{2,1,0:T(4,128)(2,1)} %param.13) | copy-start | bytes 3145732
  57.9 0.9 copy-start.5
  57.9 1.1 copy-start.13
  61.9 15.4 %copy-start.1 = (bf16[512,2048]{1,0:T(8,128)(2,1)S(1)}, bf16[512,2048]{1,0:T(8,128)(2,1)}, u32[]{:S(2)}) copy-start(bf16[512,2048]{1,0:T(8,128)(2,1)} %copy.93) | copy-start | bytes 6291460
  79.7 17.5 %collective-permute-start = (bf16[2,2,128,640]{3,2,1,0:T(8,128)(2,1)}, bf16[2,2,128,640]{3,2,1,0:T(8,128)(2,1)S(1)}, u32[]{:S(2)}, u32[]{:S(2)}) collective-permute-start(bf16[2,2,128,640]{3,2,1,0:T(8,128)(2,1)} %bitcast.16), channel_id=1, source_target_pairs={{0,1},{1,0},{2,3},{3,2},{4,5},{5,4},{6,7},{7,6},{8,9},{9,8},{10,11... | collective-permute-start | bytes 1966088 | tf_op jit(solution)/shard_map/ppermute | solution.py:87
  83.5 13.7 %all-to-all-start.2 = ((bf16[32,16,128]{2,1,0:T(8,128)(2,1)}), bf16[32,16,128]{2,1,0:T(8,128)(2,1)S(1)}, u32[]{:S(2)}, u32[]{:S(2)}) async-start(bf16[32,16,128]{2,1,0:T(8,128)(2,1)} %maximum_maximum_fusion.5), calls=%async_computation.2 | async-start | bytes 262144 | tf_op jit(solution)/shard_map/all_to_all | solution.py:88
  98.5 19.5 %collective-permute-start.2 = (bf16[2,128,640]{2,1,0:T(8,128)(2,1)S(1)}, bf16[2,128,640]{2,1,0:T(8,128)(2,1)S(1)}, u32[]{:S(2)}, u32[]{:S(2)}) collective-permute-start(bf16[2,128,640]{2,1,0:T(8,128)(2,1)S(1)} %get-tuple-element.24), channel_id=1, source_target_pairs={{0,2},{2,0},{1,3},{3,1},{4,6},{6,4},{5,7},{7,5},{8,10},{10,8},{9,1... | collective-permute-start | bytes 983048 | tf_op jit(solution)/shard_map/ppermute | solution.py:96
  100.5 14.6 %collective-permute-start.1 = (bf16[16,128]{1,0:T(8,128)(2,1)S(1)}, bf16[16,128]{1,0:T(8,128)(2,1)S(1)}, u32[]{:S(2)}, u32[]{:S(2)}) collective-permute-start(bf16[16,128]{1,0:T(8,128)(2,1)S(1)} %reduce_sum.80), channel_id=1, source_target_pairs={{0,16},{16,0},{1,17},{17,1},{2,18},{18,2},{3,19},{19,3},{4,20},{20... | collective-permute-start | bytes 12296 | tf_op jit(solution)/shard_map/ppermute | solution.py:97
  118.8 20.2 %collective-permute-start.3 = (bf16[128,640]{1,0:T(8,128)(2,1)S(1)}, bf16[128,640]{1,0:T(8,128)(2,1)S(1)}, u32[]{:S(2)}, u32[]{:S(2)}) collective-permute-start(bf16[128,640]{1,0:T(8,128)(2,1)S(1)} %get-tuple-element.30), channel_id=1, source_target_pairs={{0,4},{4,0},{1,5},{5,1},{2,6},{6,2},{3,7},{7,3},{8,12},{12,8},{9,1... | collective-permute-start | bytes 491528 | tf_op jit(solution)/shard_map/ppermute | solution.py:106
  122.0 13.4 %all-to-all-start.3 = ((bf16[32,16,128]{2,1,0:T(8,128)(2,1)}), bf16[32,16,128]{2,1,0:T(8,128)(2,1)S(1)}, u32[]{:S(2)}, u32[]{:S(2)}) async-start(bf16[32,16,128]{2,1,0:T(8,128)(2,1)} %broadcast_in_dim.39), calls=%async_computation.3 | async-start | bytes 262144 | tf_op jit(solution)/shard_map/all_to_all | solution.py:107
  142.3 5.4 %copy-start.11 = (s32[32]{0:T(128)S(1)}, s32[32]{0:T(128)}, u32[]{:S(2)}) copy-start(s32[32]{0:T(128)} %param.14) | copy-start | bytes 388
  142.5 21.6 %copy-start.10 = (f32[64,64]{1,0:T(8,128)S(1)}, f32[64,64]{1,0:T(8,128)}, u32[]{:S(2)}) copy-start(f32[64,64]{1,0:T(8,128)} %param.11) | copy-start | bytes 49156
  142.5 22.2 %copy-start.3 = (f32[512,64]{0,1:T(8,128)S(1)}, f32[512,64]{0,1:T(8,128)}, u32[]{:S(2)}) copy-start(f32[512,64]{0,1:T(8,128)} %param.10) | copy-start | bytes 393220
  142.6 22.9 %copy-start.8 = (bf16[8,32,64]{2,1,0:T(8,128)(2,1)S(1)}, bf16[8,32,64]{2,1,0:T(8,128)(2,1)}, u32[]{:S(2)}) copy-start(bf16[8,32,64]{2,1,0:T(8,128)(2,1)} %copy-done.7) | copy-start | bytes 98308
  143.5 19.3 %all-to-all-start.4 = ((bf16[8,112,128]{2,1,0:T(8,128)(2,1)}), bf16[8,112,128]{2,1,0:T(8,128)(2,1)S(1)}, u32[]{:S(2)}, u32[]{:S(2)}) async-start(bf16[8,112,128]{2,1,0:T(8,128)(2,1)} %maximum_maximum_fusion.4), calls=%async_computation.4 | async-start | bytes 458752 | tf_op jit(solution)/shard_map/all_to_all | solution.py:124
  165.5 1.3 copy-start.12

commit v2 on v0

v2 whole, which is shorter than its diff:
```python
import jax
import jax.numpy as jnp
from jax import lax
from jax.experimental import pallas as pl
from jax.experimental.pallas import tpu as pltpu
from jax.sharding import Mesh
from jax.sharding import PartitionSpec as P

HEAD_DIM = 128
KV_HEADS = 4
STEPS = 4
RANK = 64

adapter_scale = 2.0
step_length = 8.0
epsilon = 1e-06
theta_base = 1000000.0

TENSOR = ("t2", "t1", "t0")
QUAD = ("t1", "t0")
PLANE = ("y", "x", "core")
DP = ("y", "x", "zh", "core")
SWAP = [(0, 1), (1, 0)]
VMEM = pl.BlockSpec(memory_space=pltpu.VMEM)
SMALL = pltpu.CompilerParams(vmem_limit_bytes=16 * 1024 * 1024)
bf16 = jnp.bfloat16
f32 = jnp.float32


def dot(left, right, contract, precision=None):
    return lax.dot_general(
        left, right, ((contract[:1], contract[1:]), ((), ())),
        precision=precision, preferred_element_type=f32,
    )


def struct(shape, dtype):
    return jax.ShapeDtypeStruct(shape, dtype)


def partials_kernel(
    x_ref, ct_ref, at_ref, b_ref, out_ref, x_in, ct_in, at_in, b_in, sent, x_sems, sems, out_sems
):
    small = [
        pltpu.make_async_copy(source, target, sems.at[i])
        for i, (source, target) in enumerate(((at_ref, at_in), (b_ref, b_in), (ct_ref, ct_in)))
    ]
    large = [
        pltpu.make_async_copy(
            x_ref.at[pl.ds(512 * q, 512)], x_in.at[pl.ds(512 * q, 512)], x_sems.at[q]
        )
        for q in range(4)
    ]
    back = [pltpu.make_async_copy(sent.at[q], out_ref.at[q], out_sems.at[q]) for q in range(4)]
    for copy in small + large:
        copy.start()
    for copy in small:
        copy.wait()
    a = at_in[...].T.astype(bf16)
    b = b_in[...].astype(bf16)
    for q in range(4):
        sent[q, RANK:] = dot(b, ct_in[:, 512 * q : 512 * (q + 1)], (1, 0)).astype(bf16)
    for q in range(4):
        large[q].wait()
        sent[q, :RANK] = dot(x_in[512 * q : 512 * (q + 1)], a, (1, 0)).T.astype(bf16)
        back[q].start()
    for copy in back:
        copy.wait()


def partials(x, ct, at, b):
    return pl.pallas_call(
        partials_kernel,
        in_specs=[pl.BlockSpec(memory_space=pl.ANY)] * 4,
        out_specs=pl.BlockSpec(memory_space=pl.ANY),
        out_shape=struct((4, 2 * RANK, 512), bf16),
        scratch_shapes=[
            pltpu.VMEM((2048, 512), bf16),
            pltpu.VMEM((RANK, 2048), bf16),
            pltpu.VMEM((RANK, 512), f32),
            pltpu.VMEM((RANK, RANK), f32),
            pltpu.VMEM((4, 2 * RANK, 512), bf16),
            pltpu.SemaphoreType.DMA((4,)),
            pltpu.SemaphoreType.DMA((3,)),
            pltpu.SemaphoreType.DMA((4,)),
        ],
        name="partials",
    )(x, ct, at, b)


def base_kernel(me_ref, h_ref, w_ref, at_ref, send_ref, keep_ref):
    rows = h_ref[...]
    base = dot(rows, w_ref[...], (1, 0)).astype(bf16)
    acts = dot(rows, at_ref[...].T.astype(bf16), (1, 0)).T.astype(bf16)

    def write(out_ref):
        for k in range(KV_HEADS):
            out_ref[0, 128 * k : 128 * (k + 1)] = base[:, 128 * k : 128 * (k + 1)]
        out_ref[0, 512:] = acts

    @pl.when(pl.program_id(0) == 0)
    def _():
        write(send_ref)

    @pl.when(pl.program_id(0) == 1)
    def _():
        write(keep_ref)


def base_parts(me, flat, w, at):
    def rows(s, m, me_ref):
        t0 = jnp.where(s == 0, 1 - me_ref[0], me_ref[0])
        return (m % 2) * 4 + (m // 2) * 2 + t0, 0

    return pl.pallas_call(
        base_kernel,
        grid_spec=pltpu.PrefetchScalarGridSpec(
            num_scalar_prefetch=1,
            grid=(2, 4),
            in_specs=[
                pl.BlockSpec((128, 512), rows),
                pl.BlockSpec((512, 512), lambda s, m, me_ref: (0, 0)),
                pl.BlockSpec((RANK, 512), lambda s, m, me_ref: (0, 0)),
            ],
            out_specs=[
                pl.BlockSpec((1, 576, 128), lambda s, m, me_ref: (jnp.where(s == 0, m, 3), 0, 0)),
                pl.BlockSpec((1, 576, 128), lambda s, m, me_ref: (jnp.where(s == 0, 0, m), 0, 0)),
            ],
        ),
        out_shape=(struct((4, 576, 128), bf16), struct((4, 576, 128), bf16)),
        cost_estimate=pl.CostEstimate(flops=2 * 1024 * 512 * 576, bytes_accessed=3000000, transcendentals=0),
        compiler_params=SMALL,
        name="base",
    )(me, flat, w, at)


def grads_kernel(acts_ref, x_ref, ct_ref, out_ref):
    up = jnp.zeros((RANK, RANK), f32)
    for q in range(4):
        up += dot(acts_ref[q, :RANK], ct_ref[:, 512 * q : 512 * (q + 1)], (1, 1))
    folded = jnp.concatenate([up[:32], up[32:]], axis=1)
    down = jnp.zeros((RANK, 512), f32)
    for q in range(4):
        down += dot(acts_ref[q, RANK:], x_ref[512 * q : 512 * (q + 1)], (1, 0))
    for c in range(32):
        r, k = c // 4, c % 4
        tile = down[8 * r : 8 * r + 8, 128 * k : 128 * (k + 1)]
        row = jnp.broadcast_to(folded[c : c + 1], (8, 128))
        both = jnp.concatenate([tile, row], axis=0).astype(bf16)
        out_ref[c] = both


def gradients(acts, x, ct):
    return pl.pallas_call(
        grads_kernel,
        in_specs=[VMEM] * 3,
        out_specs=VMEM,
        out_shape=struct((32, 16, 128), bf16),
        compiler_params=SMALL,
        name="gradients",
    )(acts, x, ct)


def rank_kernel(got_ref, h_ref, b_ref, send_ref, down_ref, up_ref):
    for c in range(32):
        r, k = c // 4, c % 4
        both = got_ref[c].astype(f32)
        down_ref[8 * r : 8 * r + 8, 128 * k : 128 * (k + 1)] = both[:8]
        up_ref[c : c + 1] = both[8:9]
    down = down_ref[...]
    up = up_ref[...]
    square = jnp.sum(down * down) + jnp.sum(up * up)
    square = jnp.full((16, 128), square, f32)
    high = square.astype(bf16).astype(f32)
    first = lax.broadcasted_iota(jnp.int32, (16, 128), 0) < 8
    scalars = jnp.where(first, high, square - high).astype(bf16)
    low_b = b_ref[...].astype(bf16).astype(f32)
    small = jnp.concatenate(
        [up.astype(bf16), jnp.concatenate([low_b[:32], low_b[32:]], axis=1).astype(bf16), scalars],
        axis=0,
    )
    down = down.T.astype(bf16)
    for j in range(8):
        acts = dot(h_ref[128 * j : 128 * (j + 1)], down, (1, 0))
        send_ref[j, :RANK] = acts.T.astype(bf16)
        send_ref[j, RANK:] = small


def rank_parts(got, flat, b):
    return pl.pallas_call(
        rank_kernel,
        in_specs=[VMEM] * 3,
        out_specs=[VMEM] * 3,
        out_shape=(struct((8, 144, 128), bf16), struct((RANK, 512), f32), struct((32, 128), f32)),
        compiler_params=SMALL,
        name="rank",
    )(got, flat, b)


def finish_kernel(
    got_ref, kept_ref, came_ref, down_ref, up_ref, at_ref, b_ref, cos_ref, sin_ref, gain_ref,
    keys_ref, down_out_ref, up_out_ref,
):
    total = jnp.zeros((8, 128), f32)
    acts = jnp.zeros((RANK, 128), f32)
    for j in range(8):
        part = got_ref[j, 128:].astype(f32)
        total += part[:8] + part[8:]
        acts += got_ref[j, :RANK].astype(f32)
    total = total[:1] * (adapter_scale * adapter_scale)
    move = adapter_scale * (step_length / jnp.sqrt(total + epsilon))
    down_out_ref[...] = at_ref[...] - move[:, :1] * down_ref[...]
    up = up_ref[...]
    up_out_ref[...] = b_ref[...] - move[:, :RANK] * jnp.concatenate([up[:, :RANK], up[:, RANK:]], axis=0)
    base = kept_ref[...].astype(f32) + came_ref[...].astype(f32)
    rank_act = base[512:] - move * acts
    for k in range(KV_HEADS):
        pair = []
        for j in (2 * k, 2 * k + 1):
            low = got_ref[j, 96:128].astype(f32) - move * got_ref[j, 64:96].astype(f32)
            pair.append(jnp.concatenate([low[:, :RANK], low[:, RANK:]], axis=0))
        up_new = jnp.concatenate(pair, axis=1).astype(bf16).astype(f32)
        head = base[128 * k : 128 * (k + 1)] + adapter_scale * dot(
            rank_act, up_new, (0, 0), lax.Precision.HIGHEST
        )
        mean = jnp.mean(head * head, axis=-1, keepdims=True)
        head = head * lax.rsqrt(mean + epsilon) * gain_ref[...]
        turned = head * cos_ref[...] + pltpu.roll(head, 64, 1) * sin_ref[...]
        keys_ref[:, :, 128 * k : 128 * (k + 1)] = turned.reshape(32, STEPS, 128).astype(bf16)


def finish(got, kept, came, down, up, at, b, cosine, sine, gain):
    return pl.pallas_call(
        finish_kernel,
        in_specs=[VMEM] * 10,
        out_specs=[VMEM] * 3,
        out_shape=(struct((32, STEPS, 512), bf16), struct((RANK, 512), f32), struct((RANK, RANK), f32)),
        compiler_params=SMALL,
        name="finish",
    )(got, kept, came, down, up, at, b, cosine, sine, gain)


def tables(positions):
    half = HEAD_DIM // 2
    index = jnp.arange(half, dtype=f32)
    freqs = jnp.exp(-jnp.log(f32(theta_base)) * 2.0 * index / HEAD_DIM)
    places = (positions[:, None] + jnp.arange(STEPS, dtype=jnp.int32)[None, :]).astype(f32)
    angle = places.reshape(-1, 1) * freqs[None, :]
    cosine = jnp.cos(angle)
    sine = jnp.sin(angle)
    return jnp.concatenate([cosine, cosine], axis=1), jnp.concatenate([-sine, sine], axis=1)


def on_device(x, c, a, b, w, hidden, positions, gain):
    at = a.T
    ct = c.T
    flat = hidden.reshape(1024, 512)

    i0, i1, i2 = (lax.axis_index(n) for n in ("t0", "t1", "t2"))

    got = lax.all_to_all(partials(x, ct, at, b), QUAD, 0, 0)
    mine = got.astype(f32).sum(axis=0).astype(bf16)
    mine, flat = lax.optimization_barrier((mine, flat))
    other = lax.ppermute(mine, "t2", SWAP)
    sent, kept = base_parts(i0.reshape(1), flat, w, at)
    other, sent, kept = lax.optimization_barrier((other, sent, kept))
    mine = (mine.astype(f32) + other.astype(f32)).astype(bf16)
    acts = lax.all_to_all(jnp.broadcast_to(mine, (4, 128, 512)), QUAD, 0, 0)

    grads = gradients(acts, x, ct)
    grads, sent, kept = lax.optimization_barrier((grads, sent, kept))
    came = lax.ppermute(sent, "t0", SWAP)
    got = lax.all_to_all(grads, PLANE, 0, 0)
    mine = got.astype(f32).sum(axis=0).astype(bf16)
    mine, came = lax.optimization_barrier((mine, came))

    def part(i):
        pick = lambda v: lax.dynamic_index_in_dim(v.reshape(2, 2, 576, 128), i, 0, keepdims=False)
        return pick(kept) + pick(came)

    mine, sent1, kept1 = lax.optimization_barrier((mine, part(1 - i1), part(i1)))
    came1 = lax.ppermute(sent1, "t1", SWAP)
    other = lax.ppermute(mine, "zh", SWAP)
    mine = (mine.astype(f32) + other.astype(f32)).astype(bf16)
    mine, came1 = lax.optimization_barrier((mine, came1))

    def half(i):
        pick = lambda v: lax.dynamic_index_in_dim(v, i, 0, keepdims=False)
        return pick(kept1) + pick(came1)

    send, sent2, kept2 = lax.optimization_barrier(
        (jnp.broadcast_to(mine, (32, 16, 128)), half(1 - i2), half(i2))
    )
    came2 = lax.ppermute(sent2, "t2", SWAP)
    got = lax.all_to_all(send, PLANE, 0, 0)

    send, down, up = rank_parts(got, flat, b)
    send, came2 = lax.optimization_barrier((send, came2))
    got = lax.all_to_all(send, TENSOR, 0, 0)
    cosine, sine = tables(positions)
    keys, new_down, new_up = finish(got, kept2, came2, down, up, at, b, cosine, sine, gain.reshape(1, 128))
    return keys, new_down.T, new_up


def solution(mesh):
    names = ("y", "x", "zh", "core") + TENSOR
    fine = Mesh(mesh.devices.reshape(4, 4, 2, 2, 2, 2, 2), names)
    in_specs = (
        P(DP, TENSOR),
        P(DP, TENSOR),
        P(TENSOR, None),
        P(None, TENSOR),
        P(TENSOR, None),
        P(DP, None, TENSOR),
        P(DP + TENSOR),
        P(),
    )
    out_specs = (P(DP + TENSOR, None, None), P(TENSOR, None), P(None, TENSOR))
    return jax.shard_map(on_device, mesh=fine, in_specs=in_specs, out_specs=out_specs, check_vma=False)
```

time: 1420 us -> 147 us (0.10)
  blocking collectives: 691 us -> 29.4 us
  waiting for transfers between devices: 697 us -> 48.4 us
  starting transfers between devices: 0.12 us -> 52.8 us
  between operations: 16 us -> 0.83 us
    psum x3 -> x0, waiting for transfers between devices: 697 us -> none  [the longest x1 478 us: on_device(): down_gradient, up_gradient = lax.psum((down_gradient, up_gradient), 'dp')]
    psum x3 -> x0, blocking collectives: 644 us -> none  [the longest x1 497 us: on_device(): down_gradient, up_gradient = lax.psum((down_gradient, up_gradient), 'dp')]
    all_gather x1 -> x0, blocking collectives: 46.5 us -> none  [on_device(): lax.all_gather(updated_up_factor.astype(jnp.bfloat16), 'tensor', axis=1,...]
    all_to_all x0 -> x3, waiting for transfers between devices: none -> 36.6 us  [the longest x1 17.4 us: on_device(): got = lax.all_to_all(send, TENSOR, 0, 0)]
    ppermute x0 -> x5, starting transfers between devices: none -> 32.4 us  [the longest x1 12.3 us: on_device(): other = lax.ppermute(mine, 'zh', SWAP)]
    all_to_all x0 -> x2, blocking collectives: none -> 29.4 us  [the longest x1 17.4 us: on_device(): acts = lax.all_to_all(jnp.broadcast_to(mine, (4, 128, 512)), QUAD, 0, 0)]
    all_to_all x0 -> x3, starting transfers between devices: none -> 20.3 us  [the longest x1 7.59 us: on_device(): got = lax.all_to_all(grads, PLANE, 0, 0)]
  transfers between devices with their start and end apart: 3 -> 8, of which waited for: 3 -> 6; matrix products, arithmetic and copies ran while one was open for 0% -> 1% of each run, Pallas kernels for 0% -> 3%
where the time goes in v2:
time: 147 us; the launch traced here: 145 us
  starting transfers between devices  52.8 us (36%)
  waiting for transfers between devices  48.4 us (33%)
  blocking collectives  29.4 us (20%)
  Pallas kernels  10.9 us (7%)
  local copies, waits for them, and re-layouts  1.54 us (1%)
    all_to_all x1, waiting for transfers between devices, on_device(): got = lax.all_to_all(send, TENSOR, 0, 0)  17.4 us
    all_to_all x1, blocking collectives, on_device(): acts = lax.all_to_all(jnp.broadcast_to(mine, (4, 128, 512)), QUAD, 0, 0)  17.4 us
    all_to_all x1, waiting for transfers between devices, on_device(): got = lax.all_to_all(partials(x, ct, at, b), QUAD, 0, 0)  13.1 us
    ppermute x1, starting transfers between devices, on_device(): other = lax.ppermute(mine, 'zh', SWAP)  12.3 us
    all_to_all x1, blocking collectives, on_device(): got = lax.all_to_all(send, PLANE, 0, 0)  12 us
    ppermute x1, starting transfers between devices, on_device(): other = lax.ppermute(mine, 't2', SWAP)  9.1 us
    all_to_all x1, starting transfers between devices, on_device(): got = lax.all_to_all(grads, PLANE, 0, 0)  7.59 us
    all_to_all x1, starting transfers between devices, on_device(): got = lax.all_to_all(send, TENSOR, 0, 0)  6.69 us
  transfers between devices with their start and end apart: 8, of which 6 were waited for; matrix products, arithmetic and copies ran while one was open for 1% of the time, Pallas kernels for 3%

profile of v2, /device:TPU:6, one launch (start us, length us, event | category | flops | bytes accessed | tf_op | source)
XLA Modules:
  0.0 144.6 jit_solution(1085748816179213541)
XLA Ops:
  0.6 4.3 %partials.1 = bf16[4,128,512]{2,1,0:T(8,128)(2,1)} custom-call(bf16[2048,512]{1,0:T(8,128)(2,1)} %x_ref.3, bf16[64,2048]{1,0:T(8,128)(2,1)} %bitcast.15, f32[64,512]{1,0:T(8,128)} %bitcast.18, f32[64,64]{1,0:T(8,128)} %b_ref.5), custom_call_target="tpu_custom_call" | custom-call | tf_op jit(solution)/shard_map/partials/pallas_call | solution.py:72
  5.0 0.0 copy-start.2
  5.0 0.0 copy-start.5
  5.0 6.0 %all-to-all-start = ((bf16[4,128,512]{2,1,0:T(8,128)(2,1)}), bf16[4,128,512]{2,1,0:T(8,128)(2,1)S(1)}, u32[]{:S(2)}, u32[]{:S(2)}) async-start(bf16[4,128,512]{2,1,0:T(8,128)(2,1)} %partials.1), calls=%async_computation | async-start | bytes 1048576 | tf_op jit(solution)/shard_map/all_to_all | solution.py:261
  11.0 1.3 reshape.50.h_ref
  12.4 13.1 %all-to-all-done = bf16[4,128,512]{2,1,0:T(8,128)(2,1)S(1)} async-done(((bf16[4,128,512]{2,1,0:T(8,128)(2,1)}), bf16[4,128,512]{2,1,0:T(8,128)(2,1)S(1)}, u32[]{:S(2)}, u32[]{:S(2)}) %all-to-all-start) | async-done | bytes 524320 | tf_op jit(solution)/shard_map/all_to_all | solution.py:261
  25.5 0.1 reduce_sum.24
  25.6 9.1 %collective-permute-start = (bf16[128,512]{1,0:T(8,128)(2,1)S(1)}, bf16[128,512]{1,0:T(8,128)(2,1)S(1)}, u32[]{:S(2)}, u32[]{:S(2)}) collective-permute-start(bf16[128,512]{1,0:T(8,128)(2,1)S(1)} %reduce_sum.24), channel_id=1, source_target_pairs={{0,4},{4,0},{1,5},{5,1},{2,6},{6,2},{3,7},{7,3},{8,12},{12,8},{9,1... | collective-permute-start | bytes 393224 | tf_op jit(solution)/shard_map/ppermute | solution.py:264
  34.7 0.0 copy-done.2
  34.7 0.0 copy-done.5
  34.7 0.0 copy-start
  34.7 0.0 copy-start.1
  34.8 2.7 %base.1 = (bf16[4,576,128]{2,1,0:T(8,128)(2,1)S(1)}, bf16[4,576,128]{2,1,0:T(8,128)(2,1)S(1)}) custom-call(s32[1]{0:T(128)} %bitcast.2.me_ref, bf16[1024,512]{1,0:T(8,128)(2,1)S(1)} %reshape.50.h_ref, bf16[512,512]{1,0:T(8,128)(2,1)S(1)} %copy-done.5, f32[64,512]{1,0:T(8,128)S(1)} %bitcast.19), custom_call_target="tpu_custom_call" | custom-call | flops 603979776 | bytes 3000000 | tf_op jit(solution)/shard_map/base/pallas_call | solution.py:115
  37.5 6.1 %collective-permute-done = bf16[128,512]{1,0:T(8,128)(2,1)S(1)} collective-permute-done((bf16[128,512]{1,0:T(8,128)(2,1)S(1)}, bf16[128,512]{1,0:T(8,128)(2,1)S(1)}, u32[]{:S(2)}, u32[]{:S(2)}) %collective-permute-start) | collective-permute-done | bytes 131104 | tf_op jit(solution)/shard_map/ppermute | solution.py:264
  43.7 17.4 %all_to_all.25.acts_ref = bf16[4,128,512]{2,1,0:T(8,128)(2,1)S(1)} all-to-all(bf16[4,128,512]{2,1,0:T(8,128)(2,1)S(1)} %broadcast_in_dim.4), channel_id=1, replica_groups=mesh['y'=4,'x'=4,'zh'=2,'core'=2,'t2'=2,'t1'=2,'t0'=2] {'t1','t0'}, dimensions={0} | all-to-all | bytes 1048576 | tf_op jit(solution)/shard_map/all_to_all | solution.py:268
  61.1 0.0 copy-done
  61.1 0.0 copy-done.1
  61.1 1.2 gradients.1
  62.3 0.0 copy-start.3
  62.3 2.2 %collective-permute-start.1 = (bf16[4,576,128]{2,1,0:T(8,128)(2,1)S(1)}, bf16[4,576,128]{2,1,0:T(8,128)(2,1)S(1)}, u32[]{:S(2)}, u32[]{:S(2)}) collective-permute-start(bf16[4,576,128]{2,1,0:T(8,128)(2,1)S(1)} %get-tuple-element.39), channel_id=1, source_target_pairs={{0,1},{1,0},{2,3},{3,2},{4,5},{5,4},{6,7},{7,6},{8,9},{9,8},{10,11... | collective-permute-start | bytes 1769480 | tf_op jit(solution)/shard_map/ppermute | solution.py:272
  64.5 7.6 %all-to-all-start.2 = ((bf16[32,16,128]{2,1,0:T(8,128)(2,1)}), bf16[32,16,128]{2,1,0:T(8,128)(2,1)S(1)}, u32[]{:S(2)}, u32[]{:S(2)}) async-start(bf16[32,16,128]{2,1,0:T(8,128)(2,1)} %gradients.1), calls=%async_computation.2 | async-start | bytes 262144 | tf_op jit(solution)/shard_map/all_to_all | solution.py:273
  72.1 6.1 %all-to-all-done.2 = bf16[32,16,128]{2,1,0:T(8,128)(2,1)S(1)} async-done(((bf16[32,16,128]{2,1,0:T(8,128)(2,1)}), bf16[32,16,128]{2,1,0:T(8,128)(2,1)S(1)}, u32[]{:S(2)}, u32[]{:S(2)}) %all-to-all-start.2) | async-done | bytes 131104 | tf_op jit(solution)/shard_map/all_to_all | solution.py:273
  78.2 0.4 collective-permute-done.1
  78.6 0.0 copy-start.6
  78.6 0.1 add_bitcast_fusion
  78.7 0.0 copy-start.4
  78.7 3.4 %collective-permute-start.3 = (bf16[2,576,128]{2,1,0:T(8,128)(2,1)S(1)}, bf16[2,576,128]{2,1,0:T(8,128)(2,1)S(1)}, u32[]{:S(2)}, u32[]{:S(2)}) collective-permute-start(bf16[2,576,128]{2,1,0:T(8,128)(2,1)S(1)} %get-tuple-element.44), channel_id=1, source_target_pairs={{0,2},{2,0},{1,3},{3,1},{4,6},{6,4},{5,7},{7,5},{8,10},{10,8},{9,1... | collective-permute-start | bytes 884744 | tf_op jit(solution)/shard_map/ppermute | solution.py:282
  82.1 12.3 %collective-permute-start.2 = (bf16[16,128]{1,0:T(8,128)(2,1)S(1)}, bf16[16,128]{1,0:T(8,128)(2,1)S(1)}, u32[]{:S(2)}, u32[]{:S(2)}) collective-permute-start(bf16[16,128]{1,0:T(8,128)(2,1)S(1)} %reduce_sum.25), channel_id=1, source_target_pairs={{0,16},{16,0},{1,17},{17,1},{2,18},{18,2},{3,19},{19,3},{4,20},{20... | collective-permute-start | bytes 12296 | tf_op jit(solution)/shard_map/ppermute | solution.py:283
  94.4 5.3 %collective-permute-done.2 = bf16[16,128]{1,0:T(8,128)(2,1)S(1)} collective-permute-done((bf16[16,128]{1,0:T(8,128)(2,1)S(1)}, bf16[16,128]{1,0:T(8,128)(2,1)S(1)}, u32[]{:S(2)}, u32[]{:S(2)}) %collective-permute-start.2) | collective-permute-done | bytes 4128 | tf_op jit(solution)/shard_map/ppermute | solution.py:283
  99.7 0.0 collective-permute-done.3
  99.7 0.1 add_bitcast_fusion.2
  99.8 5.4 %collective-permute-start.4 = (bf16[576,128]{1,0:T(8,128)(2,1)S(1)}, bf16[576,128]{1,0:T(8,128)(2,1)S(1)}, u32[]{:S(2)}, u32[]{:S(2)}) collective-permute-start(bf16[576,128]{1,0:T(8,128)(2,1)S(1)} %get-tuple-element.50), channel_id=1, source_target_pairs={{0,4},{4,0},{1,5},{5,1},{2,6},{6,2},{3,7},{7,3},{8,12},{12,8},{9,1... | collective-permute-start | bytes 442376 | tf_op jit(solution)/shard_map/ppermute | solution.py:294
  105.3 12.0 %all_to_all.26.got_ref = bf16[32,16,128]{2,1,0:T(8,128)(2,1)S(1)} all-to-all(bf16[32,16,128]{2,1,0:T(8,128)(2,1)S(1)} %broadcast_in_dim.10), channel_id=1, replica_groups=mesh['y'=4,'x'=4,'zh'=2,'core'=2,'t2'=2,'t1'=2,'t0'=2] {'y','x','core'}, dimensions={0} | all-to-all | bytes 262144 | tf_op jit(solution)/shard_map/all_to_all | solution.py:295
  117.3 0.0 copy-done.3
  117.3 1.3 rank.1
  118.5 0.0 collective-permute-done.4.came_ref
  118.5 6.7 %all-to-all-start.4 = ((bf16[8,144,128]{2,1,0:T(8,128)(2,1)}), bf16[8,144,128]{2,1,0:T(8,128)(2,1)S(1)}, u32[]{:S(2)}, u32[]{:S(2)}) async-start(bf16[8,144,128]{2,1,0:T(8,128)(2,1)} %get-tuple-element.51), calls=%async_computation.4 | async-start | bytes 589824 | tf_op jit(solution)/shard_map/all_to_all | solution.py:299
  125.2 0.0 copy-done.6
  125.2 0.1 add_convert_fusion.1
  125.3 0.1 convert_element_type.39
  125.4 0.3 fusion
  125.7 0.1 pad_maximum_fusion
  125.9 17.4 %all-to-all-done.4.got_ref = bf16[8,144,128]{2,1,0:T(8,128)(2,1)S(1)} async-done(((bf16[8,144,128]{2,1,0:T(8,128)(2,1)}), bf16[8,144,128]{2,1,0:T(8,128)(2,1)S(1)}, u32[]{:S(2)}, u32[]{:S(2)}) %all-to-all-start.4) | async-done | bytes 294944 | tf_op jit(solution)/shard_map/all_to_all | solution.py:299
  143.2 0.0 copy-done.4
  143.2 1.4 finish.1
  (6 shorter events, 0.1 us)
Async XLA Ops:
  5.0 29.7 %copy-start.2 = (f32[512,64]{0,1:T(8,128)S(1)}, f32[512,64]{0,1:T(8,128)}, u32[]{:S(2)}) copy-start(f32[512,64]{0,1:T(8,128)} %param.10) | copy-start | bytes 393220
  5.0 29.7 %copy-start.5 = (bf16[512,512]{1,0:T(8,128)(2,1)S(1)}, bf16[512,512]{1,0:T(8,128)(2,1)}, u32[]{:S(2)}) copy-start(bf16[512,512]{1,0:T(8,128)(2,1)} %w_ref.1) | copy-start | bytes 1572868
  5.0 20.5 %all-to-all-start = ((bf16[4,128,512]{2,1,0:T(8,128)(2,1)}), bf16[4,128,512]{2,1,0:T(8,128)(2,1)S(1)}, u32[]{:S(2)}, u32[]{:S(2)}) async-start(bf16[4,128,512]{2,1,0:T(8,128)(2,1)} %partials.1), calls=%async_computation | async-start | bytes 1048576 | tf_op jit(solution)/shard_map/all_to_all | solution.py:261
  25.6 18.0 %collective-permute-start = (bf16[128,512]{1,0:T(8,128)(2,1)S(1)}, bf16[128,512]{1,0:T(8,128)(2,1)S(1)}, u32[]{:S(2)}, u32[]{:S(2)}) collective-permute-start(bf16[128,512]{1,0:T(8,128)(2,1)S(1)} %reduce_sum.24), channel_id=1, source_target_pairs={{0,4},{4,0},{1,5},{5,1},{2,6},{6,2},{3,7},{7,3},{8,12},{12,8},{9,1... | collective-permute-start | bytes 393224 | tf_op jit(solution)/shard_map/ppermute | solution.py:264
  34.7 26.3 %copy-start = (bf16[2048,512]{1,0:T(8,128)(2,1)S(1)}, bf16[2048,512]{1,0:T(8,128)(2,1)}, u32[]{:S(2)}) copy-start(bf16[2048,512]{1,0:T(8,128)(2,1)} %x_ref.3) | copy-start | bytes 6291460
  34.7 26.3 %copy-start.1 = (bf16[2048,64]{0,1:T(8,128)(2,1)S(1)}, bf16[2048,64]{0,1:T(8,128)(2,1)}, u32[]{:S(2)}) copy-start(bf16[2048,64]{0,1:T(8,128)(2,1)} %param.9) | copy-start | bytes 786436
  62.3 55.0 %copy-start.3 = (f32[64,64]{1,0:T(8,128)S(1)}, f32[64,64]{1,0:T(8,128)}, u32[]{:S(2)}) copy-start(f32[64,64]{1,0:T(8,128)} %b_ref.5) | copy-start | bytes 49156
  62.3 16.3 %collective-permute-start.1 = (bf16[4,576,128]{2,1,0:T(8,128)(2,1)S(1)}, bf16[4,576,128]{2,1,0:T(8,128)(2,1)S(1)}, u32[]{:S(2)}, u32[]{:S(2)}) collective-permute-start(bf16[4,576,128]{2,1,0:T(8,128)(2,1)S(1)} %get-tuple-element.39), channel_id=1, source_target_pairs={{0,1},{1,0},{2,3},{3,2},{4,5},{5,4},{6,7},{7,6},{8,9},{9,8},{10,11... | collective-permute-start | bytes 1769480 | tf_op jit(solution)/shard_map/ppermute | solution.py:272
  64.5 13.7 %all-to-all-start.2 = ((bf16[32,16,128]{2,1,0:T(8,128)(2,1)}), bf16[32,16,128]{2,1,0:T(8,128)(2,1)S(1)}, u32[]{:S(2)}, u32[]{:S(2)}) async-start(bf16[32,16,128]{2,1,0:T(8,128)(2,1)} %gradients.1), calls=%async_computation.2 | async-start | bytes 262144 | tf_op jit(solution)/shard_map/all_to_all | solution.py:273
  78.6 46.6 %copy-start.6 = (s32[32]{0:T(128)S(1)}, s32[32]{0:T(128)}, u32[]{:S(2)}) copy-start(s32[32]{0:T(128)} %param.14) | copy-start | bytes 388
  78.7 64.6 %copy-start.4 = (f32[128]{0:T(128)S(1)}, f32[128]{0:T(128)}, u32[]{:S(2)}) copy-start(f32[128]{0:T(128)} %param.15) | copy-start | bytes 1540
  78.7 21.1 %collective-permute-start.3 = (bf16[2,576,128]{2,1,0:T(8,128)(2,1)S(1)}, bf16[2,576,128]{2,1,0:T(8,128)(2,1)S(1)}, u32[]{:S(2)}, u32[]{:S(2)}) collective-permute-start(bf16[2,576,128]{2,1,0:T(8,128)(2,1)S(1)} %get-tuple-element.44), channel_id=1, source_target_pairs={{0,2},{2,0},{1,3},{3,1},{4,6},{6,4},{5,7},{7,5},{8,10},{10,8},{9,1... | collective-permute-start | bytes 884744 | tf_op jit(solution)/shard_map/ppermute | solution.py:282
  82.1 17.6 %collective-permute-start.2 = (bf16[16,128]{1,0:T(8,128)(2,1)S(1)}, bf16[16,128]{1,0:T(8,128)(2,1)S(1)}, u32[]{:S(2)}, u32[]{:S(2)}) collective-permute-start(bf16[16,128]{1,0:T(8,128)(2,1)S(1)} %reduce_sum.25), channel_id=1, source_target_pairs={{0,16},{16,0},{1,17},{17,1},{2,18},{18,2},{3,19},{19,3},{4,20},{20... | collective-permute-start | bytes 12296 | tf_op jit(solution)/shard_map/ppermute | solution.py:283
  99.8 18.7 %collective-permute-start.4 = (bf16[576,128]{1,0:T(8,128)(2,1)S(1)}, bf16[576,128]{1,0:T(8,128)(2,1)S(1)}, u32[]{:S(2)}, u32[]{:S(2)}) collective-permute-start(bf16[576,128]{1,0:T(8,128)(2,1)S(1)} %get-tuple-element.50), channel_id=1, source_target_pairs={{0,4},{4,0},{1,5},{5,1},{2,6},{6,2},{3,7},{7,3},{8,12},{12,8},{9,1... | collective-permute-start | bytes 442376 | tf_op jit(solution)/shard_map/ppermute | solution.py:294
  118.5 24.7 %all-to-all-start.4 = ((bf16[8,144,128]{2,1,0:T(8,128)(2,1)}), bf16[8,144,128]{2,1,0:T(8,128)(2,1)S(1)}, u32[]{:S(2)}, u32[]{:S(2)}) async-start(bf16[8,144,128]{2,1,0:T(8,128)(2,1)} %get-tuple-element.51), calls=%async_computation.4 | async-start | bytes 589824 | tf_op jit(solution)/shard_map/all_to_all | solution.py:299

commit v3 on v2

--- a/solution.py
+++ b/solution.py
@@ -271,15 +271,15 @@
     grads, sent, kept = lax.optimization_barrier((grads, sent, kept))
     came = lax.ppermute(sent, "t0", SWAP)
     got = lax.all_to_all(grads, PLANE, 0, 0)
-    mine = got.astype(f32).sum(axis=0).astype(bf16)
-    mine, came = lax.optimization_barrier((mine, came))
 
     def part(i):
         pick = lambda v: lax.dynamic_index_in_dim(v.reshape(2, 2, 576, 128), i, 0, keepdims=False)
         return pick(kept) + pick(came)
 
-    mine, sent1, kept1 = lax.optimization_barrier((mine, part(1 - i1), part(i1)))
+    sent1, kept1 = part(1 - i1), part(i1)
     came1 = lax.ppermute(sent1, "t1", SWAP)
+    got, _ = lax.optimization_barrier((got, sent1))
+    mine = got.astype(f32).sum(axis=0).astype(bf16)
     other = lax.ppermute(mine, "zh", SWAP)
     mine = (mine.astype(f32) + other.astype(f32)).astype(bf16)
     mine, came1 = lax.optimization_barrier((mine, came1))

time: 147 us -> 144 us (0.980); the launches traced: 145 us -> 143 us
  starting transfers between devices: 52.8 us -> 51.3 us
    ppermute x1, waiting for transfers between devices: 0.36 us -> 6.48 us  [on_device(): came = lax.ppermute(sent, 't0', SWAP)]
    all_to_all x1, waiting for transfers between devices: 6.08 us -> 0.01 us  [on_device(): got = lax.all_to_all(grads, PLANE, 0, 0)]
    all_to_all x1, starting transfers between devices: 6.69 us -> 5.12 us  [on_device(): got = lax.all_to_all(send, TENSOR, 0, 0)]
    ppermute x1, waiting for transfers between devices: 5.34 us -> 3.82 us  [on_device(): other = lax.ppermute(mine, 'zh', SWAP)]
  transfers between devices with their start and end apart: 8 -> 8, of which waited for: 6 -> 5; matrix products, arithmetic and copies ran while one was open for 1% -> 1% of each run, Pallas kernels for 3% -> 3%
where the time goes in v3:
time: 144 us; the launch traced here: 143 us
  starting transfers between devices  51.3 us (36%)
  waiting for transfers between devices  47 us (33%)
  blocking collectives  30.8 us (21%)
  Pallas kernels  10.9 us (8%)
  local copies, waits for them, and re-layouts  1.54 us (1%)
    all_to_all x1, waiting for transfers between devices, on_device(): got = lax.all_to_all(send, TENSOR, 0, 0)  17.4 us
    all_to_all x1, blocking collectives, on_device(): acts = lax.all_to_all(jnp.broadcast_to(mine, (4, 128, 512)), QUAD, 0, 0)  17.4 us
    all_to_all x1, blocking collectives, on_device(): got = lax.all_to_all(send, PLANE, 0, 0)  13.4 us
    all_to_all x1, waiting for transfers between devices, on_device(): got = lax.all_to_all(partials(x, ct, at, b), QUAD, 0, 0)  13.1 us
    ppermute x1, starting transfers between devices, on_device(): other = lax.ppermute(mine, 'zh', SWAP)  12.5 us
    ppermute x1, starting transfers between devices, on_device(): other = lax.ppermute(mine, 't2', SWAP)  9.1 us
    all_to_all x1, starting transfers between devices, on_device(): got = lax.all_to_all(grads, PLANE, 0, 0)  7.59 us
    ppermute x1, waiting for transfers between devices, on_device(): came = lax.ppermute(sent, 't0', SWAP)  6.48 us
  transfers between devices with their start and end apart: 8, of which 5 were waited for; matrix products, arithmetic and copies ran while one was open for 1% of the time, Pallas kernels for 3%

profile of v3, /device:TPU:6, one launch (start us, length us, event | category | flops | bytes accessed | tf_op | source)
XLA Modules:
  0.0 143.1 jit_solution(17634894357604832127)
XLA Ops:
  0.6 4.3 %partials.1 = bf16[4,128,512]{2,1,0:T(8,128)(2,1)} custom-call(bf16[2048,512]{1,0:T(8,128)(2,1)} %x_ref.3, bf16[64,2048]{1,0:T(8,128)(2,1)} %bitcast.21, f32[64,512]{1,0:T(8,128)} %bitcast.24, f32[64,64]{1,0:T(8,128)} %b_ref.5), custom_call_target="tpu_custom_call" | custom-call | tf_op jit(solution)/shard_map/partials/pallas_call | solution.py:72
  5.0 0.0 copy-start.2
  5.0 0.0 copy-start.5
  5.0 6.0 %all-to-all-start = ((bf16[4,128,512]{2,1,0:T(8,128)(2,1)}), bf16[4,128,512]{2,1,0:T(8,128)(2,1)S(1)}, u32[]{:S(2)}, u32[]{:S(2)}) async-start(bf16[4,128,512]{2,1,0:T(8,128)(2,1)} %partials.1), calls=%async_computation | async-start | bytes 1048576 | tf_op jit(solution)/shard_map/all_to_all | solution.py:261
  11.0 1.3 reshape.52.h_ref
  12.4 13.1 %all-to-all-done = bf16[4,128,512]{2,1,0:T(8,128)(2,1)S(1)} async-done(((bf16[4,128,512]{2,1,0:T(8,128)(2,1)}), bf16[4,128,512]{2,1,0:T(8,128)(2,1)S(1)}, u32[]{:S(2)}, u32[]{:S(2)}) %all-to-all-start) | async-done | bytes 524320 | tf_op jit(solution)/shard_map/all_to_all | solution.py:261
  25.5 0.1 reduce_sum.24
  25.6 9.1 %collective-permute-start = (bf16[128,512]{1,0:T(8,128)(2,1)S(1)}, bf16[128,512]{1,0:T(8,128)(2,1)S(1)}, u32[]{:S(2)}, u32[]{:S(2)}) collective-permute-start(bf16[128,512]{1,0:T(8,128)(2,1)S(1)} %reduce_sum.24), channel_id=1, source_target_pairs={{0,4},{4,0},{1,5},{5,1},{2,6},{6,2},{3,7},{7,3},{8,12},{12,8},{9,1... | collective-permute-start | bytes 393224 | tf_op jit(solution)/shard_map/ppermute | solution.py:264
  34.7 0.0 copy-done.2
  34.7 0.0 copy-done.5
  34.7 0.0 copy-start
  34.7 0.0 copy-start.1
  34.8 2.7 %base.1 = (bf16[4,576,128]{2,1,0:T(8,128)(2,1)S(1)}, bf16[4,576,128]{2,1,0:T(8,128)(2,1)S(1)}) custom-call(s32[1]{0:T(128)} %bitcast.2.me_ref, bf16[1024,512]{1,0:T(8,128)(2,1)S(1)} %reshape.52.h_ref, bf16[512,512]{1,0:T(8,128)(2,1)S(1)} %copy-done.5, f32[64,512]{1,0:T(8,128)S(1)} %bitcast.25), custom_call_target="tpu_custom_call" | custom-call | flops 603979776 | bytes 3000000 | tf_op jit(solution)/shard_map/base/pallas_call | solution.py:115
  37.5 6.1 %collective-permute-done = bf16[128,512]{1,0:T(8,128)(2,1)S(1)} collective-permute-done((bf16[128,512]{1,0:T(8,128)(2,1)S(1)}, bf16[128,512]{1,0:T(8,128)(2,1)S(1)}, u32[]{:S(2)}, u32[]{:S(2)}) %collective-permute-start) | collective-permute-done | bytes 131104 | tf_op jit(solution)/shard_map/ppermute | solution.py:264
  43.7 17.4 %all_to_all.25.acts_ref = bf16[4,128,512]{2,1,0:T(8,128)(2,1)S(1)} all-to-all(bf16[4,128,512]{2,1,0:T(8,128)(2,1)S(1)} %broadcast_in_dim.4), channel_id=1, replica_groups=mesh['y'=4,'x'=4,'zh'=2,'core'=2,'t2'=2,'t1'=2,'t0'=2] {'t1','t0'}, dimensions={0} | all-to-all | bytes 1048576 | tf_op jit(solution)/shard_map/all_to_all | solution.py:268
  61.1 0.0 copy-done
  61.1 0.0 copy-done.1
  61.1 1.2 gradients.1
  62.3 0.0 copy-start.3
  62.3 2.2 %collective-permute-start.1 = (bf16[4,576,128]{2,1,0:T(8,128)(2,1)S(1)}, bf16[4,576,128]{2,1,0:T(8,128)(2,1)S(1)}, u32[]{:S(2)}, u32[]{:S(2)}) collective-permute-start(bf16[4,576,128]{2,1,0:T(8,128)(2,1)S(1)} %get-tuple-element.36), channel_id=1, source_target_pairs={{0,1},{1,0},{2,3},{3,2},{4,5},{5,4},{6,7},{7,6},{8,9},{9,8},{10,11... | collective-permute-start | bytes 1769480 | tf_op jit(solution)/shard_map/ppermute | solution.py:272
  64.5 7.6 %all-to-all-start.2 = ((bf16[32,16,128]{2,1,0:T(8,128)(2,1)}), bf16[32,16,128]{2,1,0:T(8,128)(2,1)S(1)}, u32[]{:S(2)}, u32[]{:S(2)}) async-start(bf16[32,16,128]{2,1,0:T(8,128)(2,1)} %gradients.1), calls=%async_computation.2 | async-start | bytes 262144 | tf_op jit(solution)/shard_map/all_to_all | solution.py:273
  72.1 6.5 %collective-permute-done.1 = bf16[4,576,128]{2,1,0:T(8,128)(2,1)S(1)} collective-permute-done((bf16[4,576,128]{2,1,0:T(8,128)(2,1)S(1)}, bf16[4,576,128]{2,1,0:T(8,128)(2,1)S(1)}, u32[]{:S(2)}, u32[]{:S(2)}) %collective-permute-start.1) | collective-permute-done | bytes 589856 | tf_op jit(solution)/shard_map/ppermute | solution.py:272
  78.6 0.0 copy-start.6
  78.6 0.1 dynamic-slice_add_fusion
  78.7 0.0 copy-start.4
  78.7 2.4 %collective-permute-start.3 = (bf16[2,576,128]{2,1,0:T(8,128)(2,1)S(1)}, bf16[2,576,128]{2,1,0:T(8,128)(2,1)S(1)}, u32[]{:S(2)}, u32[]{:S(2)}) collective-permute-start(bf16[2,576,128]{2,1,0:T(8,128)(2,1)S(1)} %get-tuple-element.52), channel_id=1, source_target_pairs={{0,2},{2,0},{1,3},{3,1},{4,6},{6,4},{5,7},{7,5},{8,10},{10,8},{9,1... | collective-permute-start | bytes 884744 | tf_op jit(solution)/shard_map/ppermute | solution.py:280
  81.1 0.0 all-to-all-done.2
  81.2 12.5 %collective-permute-start.2 = (bf16[16,128]{1,0:T(8,128)(2,1)S(1)}, bf16[16,128]{1,0:T(8,128)(2,1)S(1)}, u32[]{:S(2)}, u32[]{:S(2)}) collective-permute-start(bf16[16,128]{1,0:T(8,128)(2,1)S(1)} %reduce_sum.25), channel_id=1, source_target_pairs={{0,16},{16,0},{1,17},{17,1},{2,18},{18,2},{3,19},{19,3},{4,20},{20... | collective-permute-start | bytes 12296 | tf_op jit(solution)/shard_map/ppermute | solution.py:283
  93.6 3.8 %collective-permute-done.2 = bf16[16,128]{1,0:T(8,128)(2,1)S(1)} collective-permute-done((bf16[16,128]{1,0:T(8,128)(2,1)S(1)}, bf16[16,128]{1,0:T(8,128)(2,1)S(1)}, u32[]{:S(2)}, u32[]{:S(2)}) %collective-permute-start.2) | collective-permute-done | bytes 4128 | tf_op jit(solution)/shard_map/ppermute | solution.py:283
  97.5 0.0 collective-permute-done.3
  97.5 0.1 fusion
  97.5 6.3 %collective-permute-start.4 = (bf16[576,128]{1,0:T(8,128)(2,1)S(1)}, bf16[576,128]{1,0:T(8,128)(2,1)S(1)}, u32[]{:S(2)}, u32[]{:S(2)}) collective-permute-start(bf16[576,128]{1,0:T(8,128)(2,1)S(1)} %get-tuple-element.42), channel_id=1, source_target_pairs={{0,4},{4,0},{1,5},{5,1},{2,6},{6,2},{3,7},{7,3},{8,12},{12,8},{9,1... | collective-permute-start | bytes 442376 | tf_op jit(solution)/shard_map/ppermute | solution.py:294
  103.9 13.4 %all_to_all.26.got_ref = bf16[32,16,128]{2,1,0:T(8,128)(2,1)S(1)} all-to-all(bf16[32,16,128]{2,1,0:T(8,128)(2,1)S(1)} %broadcast_in_dim.10), channel_id=1, replica_groups=mesh['y'=4,'x'=4,'zh'=2,'core'=2,'t2'=2,'t1'=2,'t0'=2] {'y','x','core'}, dimensions={0} | all-to-all | bytes 262144 | tf_op jit(solution)/shard_map/all_to_all | solution.py:295
  117.3 0.0 copy-done.3
  117.3 1.3 rank.1
  118.6 0.0 collective-permute-done.4.came_ref
  118.6 5.1 %all-to-all-start.4 = ((bf16[8,144,128]{2,1,0:T(8,128)(2,1)}), bf16[8,144,128]{2,1,0:T(8,128)(2,1)S(1)}, u32[]{:S(2)}, u32[]{:S(2)}) async-start(bf16[8,144,128]{2,1,0:T(8,128)(2,1)} %get-tuple-element.43), calls=%async_computation.4 | async-start | bytes 589824 | tf_op jit(solution)/shard_map/all_to_all | solution.py:299
  123.7 0.0 copy-done.6
  123.7 0.1 add_convert_fusion.1
  123.8 0.1 convert_element_type.39
  123.9 0.3 fusion.2
  124.2 0.1 pad_maximum_fusion
  124.3 17.4 %all-to-all-done.4.got_ref = bf16[8,144,128]{2,1,0:T(8,128)(2,1)S(1)} async-done(((bf16[8,144,128]{2,1,0:T(8,128)(2,1)}), bf16[8,144,128]{2,1,0:T(8,128)(2,1)S(1)}, u32[]{:S(2)}, u32[]{:S(2)}) %all-to-all-start.4) | async-done | bytes 294944 | tf_op jit(solution)/shard_map/all_to_all | solution.py:299
  141.7 0.0 copy-done.4
  141.7 1.4 finish.1
  (6 shorter events, 0.1 us)
Async XLA Ops:
  5.0 29.7 %copy-start.2 = (f32[512,64]{0,1:T(8,128)S(1)}, f32[512,64]{0,1:T(8,128)}, u32[]{:S(2)}) copy-start(f32[512,64]{0,1:T(8,128)} %param.10) | copy-start | bytes 393220
  5.0 29.7 %copy-start.5 = (bf16[512,512]{1,0:T(8,128)(2,1)S(1)}, bf16[512,512]{1,0:T(8,128)(2,1)}, u32[]{:S(2)}) copy-start(bf16[512,512]{1,0:T(8,128)(2,1)} %w_ref.1) | copy-start | bytes 1572868
  5.0 20.5 %all-to-all-start = ((bf16[4,128,512]{2,1,0:T(8,128)(2,1)}), bf16[4,128,512]{2,1,0:T(8,128)(2,1)S(1)}, u32[]{:S(2)}, u32[]{:S(2)}) async-start(bf16[4,128,512]{2,1,0:T(8,128)(2,1)} %partials.1), calls=%async_computation | async-start | bytes 1048576 | tf_op jit(solution)/shard_map/all_to_all | solution.py:261
  25.6 18.0 %collective-permute-start = (bf16[128,512]{1,0:T(8,128)(2,1)S(1)}, bf16[128,512]{1,0:T(8,128)(2,1)S(1)}, u32[]{:S(2)}, u32[]{:S(2)}) collective-permute-start(bf16[128,512]{1,0:T(8,128)(2,1)S(1)} %reduce_sum.24), channel_id=1, source_target_pairs={{0,4},{4,0},{1,5},{5,1},{2,6},{6,2},{3,7},{7,3},{8,12},{12,8},{9,1... | collective-permute-start | bytes 393224 | tf_op jit(solution)/shard_map/ppermute | solution.py:264
  34.7 26.3 %copy-start = (bf16[2048,512]{1,0:T(8,128)(2,1)S(1)}, bf16[2048,512]{1,0:T(8,128)(2,1)}, u32[]{:S(2)}) copy-start(bf16[2048,512]{1,0:T(8,128)(2,1)} %x_ref.3) | copy-start | bytes 6291460
  34.7 26.3 %copy-start.1 = (bf16[2048,64]{0,1:T(8,128)(2,1)S(1)}, bf16[2048,64]{0,1:T(8,128)(2,1)}, u32[]{:S(2)}) copy-start(bf16[2048,64]{0,1:T(8,128)(2,1)} %param.9) | copy-start | bytes 786436
  62.3 55.0 %copy-start.3 = (f32[64,64]{1,0:T(8,128)S(1)}, f32[64,64]{1,0:T(8,128)}, u32[]{:S(2)}) copy-start(f32[64,64]{1,0:T(8,128)} %b_ref.5) | copy-start | bytes 49156
  62.3 16.3 %collective-permute-start.1 = (bf16[4,576,128]{2,1,0:T(8,128)(2,1)S(1)}, bf16[4,576,128]{2,1,0:T(8,128)(2,1)S(1)}, u32[]{:S(2)}, u32[]{:S(2)}) collective-permute-start(bf16[4,576,128]{2,1,0:T(8,128)(2,1)S(1)} %get-tuple-element.36), channel_id=1, source_target_pairs={{0,1},{1,0},{2,3},{3,2},{4,5},{5,4},{6,7},{7,6},{8,9},{9,8},{10,11... | collective-permute-start | bytes 1769480 | tf_op jit(solution)/shard_map/ppermute | solution.py:272
  64.5 16.6 %all-to-all-start.2 = ((bf16[32,16,128]{2,1,0:T(8,128)(2,1)}), bf16[32,16,128]{2,1,0:T(8,128)(2,1)S(1)}, u32[]{:S(2)}, u32[]{:S(2)}) async-start(bf16[32,16,128]{2,1,0:T(8,128)(2,1)} %gradients.1), calls=%async_computation.2 | async-start | bytes 262144 | tf_op jit(solution)/shard_map/all_to_all | solution.py:273
  78.6 45.1 %copy-start.6 = (s32[32]{0:T(128)S(1)}, s32[32]{0:T(128)}, u32[]{:S(2)}) copy-start(s32[32]{0:T(128)} %param.14) | copy-start | bytes 388
  78.7 63.0 %copy-start.4 = (f32[128]{0:T(128)S(1)}, f32[128]{0:T(128)}, u32[]{:S(2)}) copy-start(f32[128]{0:T(128)} %param.15) | copy-start | bytes 1540
  78.7 18.8 %collective-permute-start.3 = (bf16[2,576,128]{2,1,0:T(8,128)(2,1)S(1)}, bf16[2,576,128]{2,1,0:T(8,128)(2,1)S(1)}, u32[]{:S(2)}, u32[]{:S(2)}) collective-permute-start(bf16[2,576,128]{2,1,0:T(8,128)(2,1)S(1)} %get-tuple-element.52), channel_id=1, source_target_pairs={{0,2},{2,0},{1,3},{3,1},{4,6},{6,4},{5,7},{7,5},{8,10},{10,8},{9,1... | collective-permute-start | bytes 884744 | tf_op jit(solution)/shard_map/ppermute | solution.py:280
  81.2 16.3 %collective-permute-start.2 = (bf16[16,128]{1,0:T(8,128)(2,1)S(1)}, bf16[16,128]{1,0:T(8,128)(2,1)S(1)}, u32[]{:S(2)}, u32[]{:S(2)}) collective-permute-start(bf16[16,128]{1,0:T(8,128)(2,1)S(1)} %reduce_sum.25), channel_id=1, source_target_pairs={{0,16},{16,0},{1,17},{17,1},{2,18},{18,2},{3,19},{19,3},{4,20},{20... | collective-permute-start | bytes 12296 | tf_op jit(solution)/shard_map/ppermute | solution.py:283
  97.5 21.1 %collective-permute-start.4 = (bf16[576,128]{1,0:T(8,128)(2,1)S(1)}, bf16[576,128]{1,0:T(8,128)(2,1)S(1)}, u32[]{:S(2)}, u32[]{:S(2)}) collective-permute-start(bf16[576,128]{1,0:T(8,128)(2,1)S(1)} %get-tuple-element.42), channel_id=1, source_target_pairs={{0,4},{4,0},{1,5},{5,1},{2,6},{6,2},{3,7},{7,3},{8,12},{12,8},{9,1... | collective-permute-start | bytes 442376 | tf_op jit(solution)/shard_map/ppermute | solution.py:294
  118.6 23.1 %all-to-all-start.4 = ((bf16[8,144,128]{2,1,0:T(8,128)(2,1)}), bf16[8,144,128]{2,1,0:T(8,128)(2,1)S(1)}, u32[]{:S(2)}, u32[]{:S(2)}) async-start(bf16[8,144,128]{2,1,0:T(8,128)(2,1)} %get-tuple-element.43), calls=%async_computation.4 | async-start | bytes 589824 | tf_op jit(solution)/shard_map/all_to_all | solution.py:299

commit v4 on v3

--- a/solution.py
+++ b/solution.py
@@ -22,7 +22,7 @@
 DP = ("y", "x", "zh", "core")
 SWAP = [(0, 1), (1, 0)]
 VMEM = pl.BlockSpec(memory_space=pltpu.VMEM)
-SMALL = pltpu.CompilerParams(vmem_limit_bytes=16 * 1024 * 1024)
+SMALL = pltpu.CompilerParams(vmem_limit_bytes=6 * 1024 * 1024)
 bf16 = jnp.bfloat16
 f32 = jnp.float32
 
@@ -268,7 +268,6 @@
     acts = lax.all_to_all(jnp.broadcast_to(mine, (4, 128, 512)), QUAD, 0, 0)
 
     grads = gradients(acts, x, ct)
-    grads, sent, kept = lax.optimization_barrier((grads, sent, kept))
     came = lax.ppermute(sent, "t0", SWAP)
     got = lax.all_to_all(grads, PLANE, 0, 0)
 

time: 144 us -> 144 us (level)
  blocking collectives: 30.8 us -> 11.9 us
  starting transfers between devices: 51.3 us -> 58.5 us
  waiting for transfers between devices: 47 us -> 51 us
  local copies, waits for them, and re-layouts: 1.54 us -> 4.63 us
  other arithmetic: 0.77 us -> 3.64 us
    all_to_all x1 -> x0, blocking collectives: 17.4 us -> none  [on_device(): acts = lax.all_to_all(jnp.broadcast_to(mine, (4, 128, 512)), QUAD, 0, 0)]
    all_to_all x0 -> x1, waiting for transfers between devices: none -> 11.2 us  [on_device(): acts = lax.all_to_all(jnp.broadcast_to(mine, (4, 128, 512)), QUAD, 0, 0)]
    ppermute x1, waiting for transfers between devices: 6.48 us -> 0.01 us  [on_device(): came = lax.ppermute(sent, 't0', SWAP)]
    all_to_all x0 -> x1, starting transfers between devices: none -> 4.14 us  [on_device(): acts = lax.all_to_all(jnp.broadcast_to(mine, (4, 128, 512)), QUAD, 0, 0)]
    unnamed x14 -> x22, local copies, waits for them, and re-layouts: 0.04 us -> 3.39 us
    ppermute x1, waiting for transfers between devices: 6.14 us -> 3.78 us  [on_device(): other = lax.ppermute(mine, 't2', SWAP)]
    ppermute x1, starting transfers between devices: 2.24 us -> 3.87 us  [on_device(): came = lax.ppermute(sent, 't0', SWAP)]
    all_to_all x1, waiting for transfers between devices: 0.01 us -> 1.58 us  [on_device(): got = lax.all_to_all(grads, PLANE, 0, 0)]
  transfers between devices with their start and end apart: 8 -> 9, of which waited for: 5 -> 6; matrix products, arithmetic and copies ran while one was open for 1% -> 2% of each run, Pallas kernels for 3% -> 4%
where the time goes in v4:
time: 144 us; the launch traced here: 142 us
  starting transfers between devices  58.5 us (41%)
  waiting for transfers between devices  51 us (35%)
  blocking collectives  11.9 us (8%)
  Pallas kernels  11.4 us (8%)
  local copies, waits for them, and re-layouts  4.63 us (3%)
  other arithmetic  3.64 us (3%)
    all_to_all x1, waiting for transfers between devices, on_device(): got = lax.all_to_all(send, TENSOR, 0, 0)  17.4 us
    all_to_all x1, waiting for transfers between devices, on_device(): got = lax.all_to_all(partials(x, ct, at, b), QUAD, 0, 0)  14.2 us
    ppermute x1, starting transfers between devices, on_device(): other = lax.ppermute(mine, 'zh', SWAP)  12.3 us
    all_to_all x1, blocking collectives, on_device(): got = lax.all_to_all(send, PLANE, 0, 0)  11.9 us
    all_to_all x1, waiting for transfers between devices, on_device(): acts = lax.all_to_all(jnp.broadcast_to(mine, (4, 128, 512)), QUAD, 0, 0)  11.2 us
    ppermute x1, starting transfers between devices, on_device(): other = lax.ppermute(mine, 't2', SWAP)  9.08 us
    all_to_all x1, starting transfers between devices, on_device(): got = lax.all_to_all(grads, PLANE, 0, 0)  7.7 us
    all_to_all x1, starting transfers between devices, on_device(): got = lax.all_to_all(send, TENSOR, 0, 0)  6.31 us
  transfers between devices with their start and end apart: 9, of which 6 were waited for; matrix products, arithmetic and copies ran while one was open for 2% of the time, Pallas kernels for 4%

profile of v4, /device:TPU:6, one launch (start us, length us, event | category | flops | bytes accessed | tf_op | source)
XLA Modules:
  0.0 142.0 jit_solution(16577986322897125785)
XLA Ops:
  0.6 0.0 copy-start.9
  0.6 4.4 %partials.1 = bf16[4,128,512]{2,1,0:T(8,128)(2,1)} custom-call(bf16[2048,512]{1,0:T(8,128)(2,1)} %x_ref.3, bf16[64,2048]{1,0:T(8,128)(2,1)} %bitcast.21, f32[64,512]{1,0:T(8,128)} %bitcast.24, f32[64,64]{1,0:T(8,128)} %b_ref.5), custom_call_target="tpu_custom_call" | custom-call | tf_op jit(solution)/shard_map/partials/pallas_call | solution.py:72
  5.1 0.0 copy-start.3
  5.1 6.0 %all-to-all-start = ((bf16[4,128,512]{2,1,0:T(8,128)(2,1)}), bf16[4,128,512]{2,1,0:T(8,128)(2,1)S(1)}, u32[]{:S(2)}, u32[]{:S(2)}) async-start(bf16[4,128,512]{2,1,0:T(8,128)(2,1)} %partials.1), calls=%async_computation | async-start | bytes 1048576 | tf_op jit(solution)/shard_map/all_to_all | solution.py:261
  11.1 0.0 copy-done.9
  11.1 0.3 reshape.52.h_ref
  11.4 14.2 %all-to-all-done = bf16[4,128,512]{2,1,0:T(8,128)(2,1)S(1)} async-done(((bf16[4,128,512]{2,1,0:T(8,128)(2,1)}), bf16[4,128,512]{2,1,0:T(8,128)(2,1)S(1)}, u32[]{:S(2)}, u32[]{:S(2)}) %all-to-all-start) | async-done | bytes 524320 | tf_op jit(solution)/shard_map/all_to_all | solution.py:261
  25.6 0.7 reduce_sum.24
  26.4 9.1 %collective-permute-start = (bf16[128,512]{1,0:T(8,128)(2,1)}, bf16[128,512]{1,0:T(8,128)(2,1)}, u32[]{:S(2)}, u32[]{:S(2)}) collective-permute-start(bf16[128,512]{1,0:T(8,128)(2,1)} %reduce_sum.24), channel_id=1, source_target_pairs={{0,4},{4,0},{1,5},{5,1},{2,6},{6,2},{3,7},{7,3},{8,12},{12,8},{9,1... | collective-permute-start | bytes 393224 | tf_op jit(solution)/shard_map/ppermute | solution.py:264
  35.4 0.0 copy-done.3
  35.5 0.0 copy-start.8
  35.5 1.0 copy-done.8
  36.5 0.0 copy-start
  36.5 0.0 copy-start.1
  36.5 2.7 %base.1 = (bf16[4,576,128]{2,1,0:T(8,128)(2,1)S(1)}, bf16[4,576,128]{2,1,0:T(8,128)(2,1)S(1)}) custom-call(s32[1]{0:T(128)} %bitcast.2.me_ref, bf16[1024,512]{1,0:T(8,128)(2,1)S(1)} %reshape.52.h_ref, bf16[512,512]{1,0:T(8,128)(2,1)S(1)} %copy-done.8, f32[64,512]{1,0:T(8,128)S(1)} %bitcast.25), custom_call_target="tpu_custom_call" | custom-call | flops 603979776 | bytes 3000000 | tf_op jit(solution)/shard_map/base/pallas_call | solution.py:115
  39.2 0.0 copy-start.2
  39.2 0.8 copy-done.2
  40.1 0.0 copy-start.7
  40.1 0.8 copy-done.7
  40.9 3.8 %collective-permute-done = bf16[128,512]{1,0:T(8,128)(2,1)} collective-permute-done((bf16[128,512]{1,0:T(8,128)(2,1)}, bf16[128,512]{1,0:T(8,128)(2,1)}, u32[]{:S(2)}, u32[]{:S(2)}) %collective-permute-start) | collective-permute-done | bytes 131104 | tf_op jit(solution)/shard_map/ppermute | solution.py:264
  44.7 1.0 add_convert_fusion
  45.7 0.8 broadcast_in_dim.4
  46.5 4.1 %all-to-all-start.1 = ((bf16[4,128,512]{2,1,0:T(8,128)(2,1)}), bf16[4,128,512]{2,1,0:T(8,128)(2,1)}, u32[]{:S(2)}, u32[]{:S(2)}) async-start(bf16[4,128,512]{2,1,0:T(8,128)(2,1)} %broadcast_in_dim.4), calls=%async_computation.1 | async-start | bytes 1048576 | tf_op jit(solution)/shard_map/all_to_all | solution.py:268
  50.7 3.9 %collective-permute-start.1 = (bf16[4,576,128]{2,1,0:T(8,128)(2,1)}, bf16[4,576,128]{2,1,0:T(8,128)(2,1)}, u32[]{:S(2)}, u32[]{:S(2)}) collective-permute-start(bf16[4,576,128]{2,1,0:T(8,128)(2,1)} %copy-done.7), channel_id=1, source_target_pairs={{0,1},{1,0},{2,3},{3,2},{4,5},{5,4},{6,7},{7,6},{8,9},{9,8},{10,11... | collective-permute-start | bytes 1769480 | tf_op jit(solution)/shard_map/ppermute | solution.py:271
  54.6 11.2 %all-to-all-done.1.acts_ref = bf16[4,128,512]{2,1,0:T(8,128)(2,1)} async-done(((bf16[4,128,512]{2,1,0:T(8,128)(2,1)}), bf16[4,128,512]{2,1,0:T(8,128)(2,1)}, u32[]{:S(2)}, u32[]{:S(2)}) %all-to-all-start.1) | async-done | bytes 524320 | tf_op jit(solution)/shard_map/all_to_all | solution.py:268
  65.8 0.0 copy-done
  65.8 0.0 copy-done.1
  65.8 1.6 %gradients.1 = bf16[32,16,128]{2,1,0:T(8,128)(2,1)S(1)} custom-call(bf16[4,128,512]{2,1,0:T(8,128)(2,1)} %all-to-all-done.1.acts_ref, bf16[2048,512]{1,0:T(8,128)(2,1)S(1)} %copy-done, bf16[64,2048]{1,0:T(8,128)(2,1)S(1)} %bitcast.22), custom_call_target="tpu_custom_call" | custom-call | tf_op jit(solution)/shard_map/gradients/pallas_call | solution.py:154
  67.4 0.0 copy-start.4
  67.4 0.7 copy-done.4
  68.1 0.0 copy-start.5
  68.1 7.7 %all-to-all-start.2 = ((bf16[32,16,128]{2,1,0:T(8,128)(2,1)}), bf16[32,16,128]{2,1,0:T(8,128)(2,1)S(1)}, u32[]{:S(2)}, u32[]{:S(2)}) async-start(bf16[32,16,128]{2,1,0:T(8,128)(2,1)} %copy-done.4), calls=%async_computation.2 | async-start | bytes 262144 | tf_op jit(solution)/shard_map/all_to_all | solution.py:272
  75.8 0.0 collective-permute-done.1
  75.8 0.0 copy-start.10
  75.8 1.3 dynamic-slice_add_fusion
  77.1 0.0 copy-start.6
  77.1 3.2 %collective-permute-start.3 = (bf16[2,576,128]{2,1,0:T(8,128)(2,1)S(1)}, bf16[2,576,128]{2,1,0:T(8,128)(2,1)S(1)}, u32[]{:S(2)}, u32[]{:S(2)}) collective-permute-start(bf16[2,576,128]{2,1,0:T(8,128)(2,1)S(1)} %get-tuple-element.46), channel_id=1, source_target_pairs={{0,2},{2,0},{1,3},{3,1},{4,6},{6,4},{5,7},{7,5},{8,10},{10,8},{9,1... | collective-permute-start | bytes 884744 | tf_op jit(solution)/shard_map/ppermute | solution.py:279
  80.3 1.6 %all-to-all-done.2 = bf16[32,16,128]{2,1,0:T(8,128)(2,1)S(1)} async-done(((bf16[32,16,128]{2,1,0:T(8,128)(2,1)}), bf16[32,16,128]{2,1,0:T(8,128)(2,1)S(1)}, u32[]{:S(2)}, u32[]{:S(2)}) %all-to-all-start.2) | async-done | bytes 131104 | tf_op jit(solution)/shard_map/all_to_all | solution.py:272
  81.9 12.3 %collective-permute-start.2 = (bf16[16,128]{1,0:T(8,128)(2,1)S(1)}, bf16[16,128]{1,0:T(8,128)(2,1)S(1)}, u32[]{:S(2)}, u32[]{:S(2)}) collective-permute-start(bf16[16,128]{1,0:T(8,128)(2,1)S(1)} %reduce_sum.25), channel_id=1, source_target_pairs={{0,16},{16,0},{1,17},{17,1},{2,18},{18,2},{3,19},{19,3},{4,20},{20... | collective-permute-start | bytes 12296 | tf_op jit(solution)/shard_map/ppermute | solution.py:282
  94.2 2.8 %collective-permute-done.2 = bf16[16,128]{1,0:T(8,128)(2,1)S(1)} collective-permute-done((bf16[16,128]{1,0:T(8,128)(2,1)S(1)}, bf16[16,128]{1,0:T(8,128)(2,1)S(1)}, u32[]{:S(2)}, u32[]{:S(2)}) %collective-permute-start.2) | collective-permute-done | bytes 4128 | tf_op jit(solution)/shard_map/ppermute | solution.py:282
  97.1 0.0 collective-permute-done.3
  97.1 0.1 fusion
  97.2 5.9 %collective-permute-start.4 = (bf16[576,128]{1,0:T(8,128)(2,1)S(1)}, bf16[576,128]{1,0:T(8,128)(2,1)S(1)}, u32[]{:S(2)}, u32[]{:S(2)}) collective-permute-start(bf16[576,128]{1,0:T(8,128)(2,1)S(1)} %get-tuple-element.36), channel_id=1, source_target_pairs={{0,4},{4,0},{1,5},{5,1},{2,6},{6,2},{3,7},{7,3},{8,12},{12,8},{9,1... | collective-permute-start | bytes 442376 | tf_op jit(solution)/shard_map/ppermute | solution.py:293
  103.1 11.9 %all_to_all.25.got_ref = bf16[32,16,128]{2,1,0:T(8,128)(2,1)S(1)} all-to-all(bf16[32,16,128]{2,1,0:T(8,128)(2,1)S(1)} %broadcast_in_dim.10), channel_id=1, replica_groups=mesh['y'=4,'x'=4,'zh'=2,'core'=2,'t2'=2,'t1'=2,'t0'=2] {'y','x','core'}, dimensions={0} | all-to-all | bytes 262144 | tf_op jit(solution)/shard_map/all_to_all | solution.py:294
  115.0 0.0 copy-done.5
  115.0 1.3 rank.1
  116.3 0.0 collective-permute-done.4.came_ref
  116.3 6.3 %all-to-all-start.4 = ((bf16[8,144,128]{2,1,0:T(8,128)(2,1)}), bf16[8,144,128]{2,1,0:T(8,128)(2,1)S(1)}, u32[]{:S(2)}, u32[]{:S(2)}) async-start(bf16[8,144,128]{2,1,0:T(8,128)(2,1)} %get-tuple-element.37), calls=%async_computation.4 | async-start | bytes 589824 | tf_op jit(solution)/shard_map/all_to_all | solution.py:298
  122.6 0.0 copy-done.10
  122.6 0.1 add_convert_fusion.1
  122.7 0.1 convert_element_type.39
  122.8 0.3 fusion.2
  123.1 0.1 pad_maximum_fusion
  123.3 17.4 %all-to-all-done.4.got_ref = bf16[8,144,128]{2,1,0:T(8,128)(2,1)S(1)} async-done(((bf16[8,144,128]{2,1,0:T(8,128)(2,1)}), bf16[8,144,128]{2,1,0:T(8,128)(2,1)S(1)}, u32[]{:S(2)}, u32[]{:S(2)}) %all-to-all-start.4) | async-done | bytes 294944 | tf_op jit(solution)/shard_map/all_to_all | solution.py:298
  140.6 0.0 copy-done.6
  140.6 1.4 finish.1
  (4 shorter events, 0.1 us)
Async XLA Ops:
  0.6 10.5 %copy-start.9 = (bf16[256,4,512]{2,1,0:T(4,128)(2,1)S(1)}, bf16[256,4,512]{2,1,0:T(4,128)(2,1)}, u32[]{:S(2)}) copy-start(bf16[256,4,512]{2,1,0:T(4,128)(2,1)} %param.13) | copy-start | bytes 3145732
  5.1 30.4 %copy-start.3 = (f32[512,64]{0,1:T(8,128)S(1)}, f32[512,64]{0,1:T(8,128)}, u32[]{:S(2)}) copy-start(f32[512,64]{0,1:T(8,128)} %param.10) | copy-start | bytes 393220
  5.1 20.5 %all-to-all-start = ((bf16[4,128,512]{2,1,0:T(8,128)(2,1)}), bf16[4,128,512]{2,1,0:T(8,128)(2,1)S(1)}, u32[]{:S(2)}, u32[]{:S(2)}) async-start(bf16[4,128,512]{2,1,0:T(8,128)(2,1)} %partials.1), calls=%async_computation | async-start | bytes 1048576 | tf_op jit(solution)/shard_map/all_to_all | solution.py:261
  26.4 18.3 %collective-permute-start = (bf16[128,512]{1,0:T(8,128)(2,1)}, bf16[128,512]{1,0:T(8,128)(2,1)}, u32[]{:S(2)}, u32[]{:S(2)}) collective-permute-start(bf16[128,512]{1,0:T(8,128)(2,1)} %reduce_sum.24), channel_id=1, source_target_pairs={{0,4},{4,0},{1,5},{5,1},{2,6},{6,2},{3,7},{7,3},{8,12},{12,8},{9,1... | collective-permute-start | bytes 393224 | tf_op jit(solution)/shard_map/ppermute | solution.py:264
  35.5 1.0 copy-start.8
  36.5 29.3 %copy-start = (bf16[2048,512]{1,0:T(8,128)(2,1)S(1)}, bf16[2048,512]{1,0:T(8,128)(2,1)}, u32[]{:S(2)}) copy-start(bf16[2048,512]{1,0:T(8,128)(2,1)} %x_ref.3) | copy-start | bytes 6291460
  36.5 29.3 %copy-start.1 = (bf16[2048,64]{0,1:T(8,128)(2,1)S(1)}, bf16[2048,64]{0,1:T(8,128)(2,1)}, u32[]{:S(2)}) copy-start(bf16[2048,64]{0,1:T(8,128)(2,1)} %param.9) | copy-start | bytes 786436
  39.2 0.8 copy-start.2
  40.1 0.8 copy-start.7
  46.5 19.3 %all-to-all-start.1 = ((bf16[4,128,512]{2,1,0:T(8,128)(2,1)}), bf16[4,128,512]{2,1,0:T(8,128)(2,1)}, u32[]{:S(2)}, u32[]{:S(2)}) async-start(bf16[4,128,512]{2,1,0:T(8,128)(2,1)} %broadcast_in_dim.4), calls=%async_computation.1 | async-start | bytes 1048576 | tf_op jit(solution)/shard_map/all_to_all | solution.py:268
  50.7 25.1 %collective-permute-start.1 = (bf16[4,576,128]{2,1,0:T(8,128)(2,1)}, bf16[4,576,128]{2,1,0:T(8,128)(2,1)}, u32[]{:S(2)}, u32[]{:S(2)}) collective-permute-start(bf16[4,576,128]{2,1,0:T(8,128)(2,1)} %copy-done.7), channel_id=1, source_target_pairs={{0,1},{1,0},{2,3},{3,2},{4,5},{5,4},{6,7},{7,6},{8,9},{9,8},{10,11... | collective-permute-start | bytes 1769480 | tf_op jit(solution)/shard_map/ppermute | solution.py:271
  67.4 0.7 copy-start.4
  68.1 47.0 %copy-start.5 = (f32[64,64]{1,0:T(8,128)S(1)}, f32[64,64]{1,0:T(8,128)}, u32[]{:S(2)}) copy-start(f32[64,64]{1,0:T(8,128)} %b_ref.5) | copy-start | bytes 49156
  68.1 13.8 %all-to-all-start.2 = ((bf16[32,16,128]{2,1,0:T(8,128)(2,1)}), bf16[32,16,128]{2,1,0:T(8,128)(2,1)S(1)}, u32[]{:S(2)}, u32[]{:S(2)}) async-start(bf16[32,16,128]{2,1,0:T(8,128)(2,1)} %copy-done.4), calls=%async_computation.2 | async-start | bytes 262144 | tf_op jit(solution)/shard_map/all_to_all | solution.py:272
  75.8 46.8 %copy-start.10 = (s32[32]{0:T(128)S(1)}, s32[32]{0:T(128)}, u32[]{:S(2)}) copy-start(s32[32]{0:T(128)} %param.14) | copy-start | bytes 388
  77.1 63.5 %copy-start.6 = (f32[128]{0:T(128)S(1)}, f32[128]{0:T(128)}, u32[]{:S(2)}) copy-start(f32[128]{0:T(128)} %param.15) | copy-start | bytes 1540
  77.1 20.0 %collective-permute-start.3 = (bf16[2,576,128]{2,1,0:T(8,128)(2,1)S(1)}, bf16[2,576,128]{2,1,0:T(8,128)(2,1)S(1)}, u32[]{:S(2)}, u32[]{:S(2)}) collective-permute-start(bf16[2,576,128]{2,1,0:T(8,128)(2,1)S(1)} %get-tuple-element.46), channel_id=1, source_target_pairs={{0,2},{2,0},{1,3},{3,1},{4,6},{6,4},{5,7},{7,5},{8,10},{10,8},{9,1... | collective-permute-start | bytes 884744 | tf_op jit(solution)/shard_map/ppermute | solution.py:279
  81.9 15.2 %collective-permute-start.2 = (bf16[16,128]{1,0:T(8,128)(2,1)S(1)}, bf16[16,128]{1,0:T(8,128)(2,1)S(1)}, u32[]{:S(2)}, u32[]{:S(2)}) collective-permute-start(bf16[16,128]{1,0:T(8,128)(2,1)S(1)} %reduce_sum.25), channel_id=1, source_target_pairs={{0,16},{16,0},{1,17},{17,1},{2,18},{18,2},{3,19},{19,3},{4,20},{20... | collective-permute-start | bytes 12296 | tf_op jit(solution)/shard_map/ppermute | solution.py:282
  97.2 19.1 %collective-permute-start.4 = (bf16[576,128]{1,0:T(8,128)(2,1)S(1)}, bf16[576,128]{1,0:T(8,128)(2,1)S(1)}, u32[]{:S(2)}, u32[]{:S(2)}) collective-permute-start(bf16[576,128]{1,0:T(8,128)(2,1)S(1)} %get-tuple-element.36), channel_id=1, source_target_pairs={{0,4},{4,0},{1,5},{5,1},{2,6},{6,2},{3,7},{7,3},{8,12},{12,8},{9,1... | collective-permute-start | bytes 442376 | tf_op jit(solution)/shard_map/ppermute | solution.py:293
  116.3 24.3 %all-to-all-start.4 = ((bf16[8,144,128]{2,1,0:T(8,128)(2,1)}), bf16[8,144,128]{2,1,0:T(8,128)(2,1)S(1)}, u32[]{:S(2)}, u32[]{:S(2)}) async-start(bf16[8,144,128]{2,1,0:T(8,128)(2,1)} %get-tuple-element.37), calls=%async_computation.4 | async-start | bytes 589824 | tf_op jit(solution)/shard_map/all_to_all | solution.py:298

commit v5 on v4

--- a/solution.py
+++ b/solution.py
@@ -260,9 +260,9 @@
 
     got = lax.all_to_all(partials(x, ct, at, b), QUAD, 0, 0)
     mine = got.astype(f32).sum(axis=0).astype(bf16)
-    mine, flat = lax.optimization_barrier((mine, flat))
+    sent, kept = base_parts(i0.reshape(1), flat, w, at)
+    mine, sent, kept = lax.optimization_barrier((mine, sent, kept))
     other = lax.ppermute(mine, "t2", SWAP)
-    sent, kept = base_parts(i0.reshape(1), flat, w, at)
     other, sent, kept = lax.optimization_barrier((other, sent, kept))
     mine = (mine.astype(f32) + other.astype(f32)).astype(bf16)
     acts = lax.all_to_all(jnp.broadcast_to(mine, (4, 128, 512)), QUAD, 0, 0)

time: 144 us -> 145 us (level)
    all_to_all x1, waiting for transfers between devices: 14.2 us -> 8.87 us  [on_device(): got = lax.all_to_all(partials(x, ct, at, b), QUAD, 0, 0)]
    ppermute x1, waiting for transfers between devices: 3.78 us -> 9.03 us  [on_device(): other = lax.ppermute(mine, 't2', SWAP)]
where the time goes in v5:
time: 145 us; the launch traced here: 143 us
  starting transfers between devices  58.6 us (40%)
  waiting for transfers between devices  51 us (35%)
  blocking collectives  12 us (8%)
  Pallas kernels  11.4 us (8%)
  other arithmetic  4.64 us (3%)
  local copies, waits for them, and re-layouts  4.63 us (3%)
    all_to_all x1, waiting for transfers between devices, on_device(): got = lax.all_to_all(send, TENSOR, 0, 0)  17.4 us
    ppermute x1, starting transfers between devices, on_device(): other = lax.ppermute(mine, 'zh', SWAP)  13.1 us
    all_to_all x1, blocking collectives, on_device(): got = lax.all_to_all(send, PLANE, 0, 0)  12 us
    all_to_all x1, waiting for transfers between devices, on_device(): acts = lax.all_to_all(jnp.broadcast_to(mine, (4, 128, 512)), QUAD, 0, 0)  11.2 us
    ppermute x1, starting transfers between devices, on_device(): other = lax.ppermute(mine, 't2', SWAP)  9.07 us
    ppermute x1, waiting for transfers between devices, on_device(): other = lax.ppermute(mine, 't2', SWAP)  9.03 us
    all_to_all x1, waiting for transfers between devices, on_device(): got = lax.all_to_all(partials(x, ct, at, b), QUAD, 0, 0)  8.87 us
    all_to_all x1, starting transfers between devices, on_device(): got = lax.all_to_all(grads, PLANE, 0, 0)  7.7 us
  transfers between devices with their start and end apart: 9, of which 6 were waited for; matrix products, arithmetic and copies ran while one was open for 2% of the time, Pallas kernels for 4%

profile of v5, /device:TPU:6, one launch (start us, length us, event | category | flops | bytes accessed | tf_op | source)
XLA Modules:
  0.0 143.0 jit_solution(12304398520778472399)
XLA Ops:
  0.6 0.0 copy-start.9
  0.6 4.4 %partials.1 = bf16[4,128,512]{2,1,0:T(8,128)(2,1)} custom-call(bf16[2048,512]{1,0:T(8,128)(2,1)} %x_ref.3, bf16[64,2048]{1,0:T(8,128)(2,1)} %bitcast.21, f32[64,512]{1,0:T(8,128)} %bitcast.24, f32[64,64]{1,0:T(8,128)} %b_ref.5), custom_call_target="tpu_custom_call" | custom-call | tf_op jit(solution)/shard_map/partials/pallas_call | solution.py:72
  5.1 0.0 copy-start.3
  5.1 6.0 %all-to-all-start = ((bf16[4,128,512]{2,1,0:T(8,128)(2,1)}), bf16[4,128,512]{2,1,0:T(8,128)(2,1)}, u32[]{:S(2)}, u32[]{:S(2)}) async-start(bf16[4,128,512]{2,1,0:T(8,128)(2,1)} %partials.1), calls=%async_computation | async-start | bytes 1048576 | tf_op jit(solution)/shard_map/all_to_all | solution.py:261
  11.1 0.0 copy-done.9
  11.1 0.3 reshape.53.h_ref
  11.4 0.0 copy-done.3
  11.4 0.0 copy-start.8
  11.4 1.0 copy-done.8
  12.5 0.0 copy-start
  12.5 0.0 copy-start.1
  12.5 2.7 %base.1 = (bf16[4,576,128]{2,1,0:T(8,128)(2,1)S(1)}, bf16[4,576,128]{2,1,0:T(8,128)(2,1)S(1)}) custom-call(s32[1]{0:T(128)} %bitcast.2.me_ref, bf16[1024,512]{1,0:T(8,128)(2,1)S(1)} %reshape.53.h_ref, bf16[512,512]{1,0:T(8,128)(2,1)S(1)} %copy-done.8, f32[64,512]{1,0:T(8,128)S(1)} %bitcast.25), custom_call_target="tpu_custom_call" | custom-call | flops 603979776 | bytes 3000000 | tf_op jit(solution)/shard_map/base/pallas_call | solution.py:115
  15.2 0.0 copy-start.2
  15.2 0.8 copy-done.2
  16.0 0.0 copy-start.7
  16.0 0.8 copy-done.7
  16.9 8.9 %all-to-all-done = bf16[4,128,512]{2,1,0:T(8,128)(2,1)} async-done(((bf16[4,128,512]{2,1,0:T(8,128)(2,1)}), bf16[4,128,512]{2,1,0:T(8,128)(2,1)}, u32[]{:S(2)}, u32[]{:S(2)}) %all-to-all-start) | async-done | bytes 524320 | tf_op jit(solution)/shard_map/all_to_all | solution.py:261
  25.7 1.8 %reduce_sum.24 = bf16[128,512]{1,0:T(8,128)(2,1)} reduce(bf16[4,128,512]{2,1,0:T(8,128)(2,1)} %all-to-all-done, bf16[]{:T(256)} %constant.40.clone.1), dimensions={0}, to_apply=%region_0.0 | reduce | flops 196608 | bytes 655362 | tf_op jit(solution)/shard_map/reduce_sum | solution.py:262
  27.5 9.1 %collective-permute-start = (bf16[128,512]{1,0:T(8,128)(2,1)}, bf16[128,512]{1,0:T(8,128)(2,1)S(1)}, u32[]{:S(2)}, u32[]{:S(2)}) collective-permute-start(bf16[128,512]{1,0:T(8,128)(2,1)} %reduce_sum.24), channel_id=1, source_target_pairs={{0,4},{4,0},{1,5},{5,1},{2,6},{6,2},{3,7},{7,3},{8,12},{12,8},{9,1... | collective-permute-start | bytes 393224 | tf_op jit(solution)/shard_map/ppermute | solution.py:265
  36.6 9.0 %collective-permute-done = bf16[128,512]{1,0:T(8,128)(2,1)S(1)} collective-permute-done((bf16[128,512]{1,0:T(8,128)(2,1)}, bf16[128,512]{1,0:T(8,128)(2,1)S(1)}, u32[]{:S(2)}, u32[]{:S(2)}) %collective-permute-start) | collective-permute-done | bytes 131104 | tf_op jit(solution)/shard_map/ppermute | solution.py:265
  45.6 0.9 add_convert_fusion
  46.6 0.8 broadcast_in_dim.4
  47.4 4.1 %all-to-all-start.1 = ((bf16[4,128,512]{2,1,0:T(8,128)(2,1)}), bf16[4,128,512]{2,1,0:T(8,128)(2,1)}, u32[]{:S(2)}, u32[]{:S(2)}) async-start(bf16[4,128,512]{2,1,0:T(8,128)(2,1)} %broadcast_in_dim.4), calls=%async_computation.1 | async-start | bytes 1048576 | tf_op jit(solution)/shard_map/all_to_all | solution.py:268
  51.6 3.9 %collective-permute-start.1 = (bf16[4,576,128]{2,1,0:T(8,128)(2,1)}, bf16[4,576,128]{2,1,0:T(8,128)(2,1)}, u32[]{:S(2)}, u32[]{:S(2)}) collective-permute-start(bf16[4,576,128]{2,1,0:T(8,128)(2,1)} %copy-done.7), channel_id=1, source_target_pairs={{0,1},{1,0},{2,3},{3,2},{4,5},{5,4},{6,7},{7,6},{8,9},{9,8},{10,11... | collective-permute-start | bytes 1769480 | tf_op jit(solution)/shard_map/ppermute | solution.py:271
  55.5 11.2 %all-to-all-done.1.acts_ref = bf16[4,128,512]{2,1,0:T(8,128)(2,1)} async-done(((bf16[4,128,512]{2,1,0:T(8,128)(2,1)}), bf16[4,128,512]{2,1,0:T(8,128)(2,1)}, u32[]{:S(2)}, u32[]{:S(2)}) %all-to-all-start.1) | async-done | bytes 524320 | tf_op jit(solution)/shard_map/all_to_all | solution.py:268
  66.7 0.0 copy-done
  66.7 0.0 copy-done.1
  66.7 1.6 %gradients.1 = bf16[32,16,128]{2,1,0:T(8,128)(2,1)S(1)} custom-call(bf16[4,128,512]{2,1,0:T(8,128)(2,1)} %all-to-all-done.1.acts_ref, bf16[2048,512]{1,0:T(8,128)(2,1)S(1)} %copy-done, bf16[64,2048]{1,0:T(8,128)(2,1)S(1)} %bitcast.22), custom_call_target="tpu_custom_call" | custom-call | tf_op jit(solution)/shard_map/gradients/pallas_call | solution.py:154
  68.3 0.0 copy-start.4
  68.3 0.7 copy-done.4
  69.0 0.0 copy-start.5
  69.0 7.7 %all-to-all-start.2 = ((bf16[32,16,128]{2,1,0:T(8,128)(2,1)}), bf16[32,16,128]{2,1,0:T(8,128)(2,1)S(1)}, u32[]{:S(2)}, u32[]{:S(2)}) async-start(bf16[32,16,128]{2,1,0:T(8,128)(2,1)} %copy-done.4), calls=%async_computation.2 | async-start | bytes 262144 | tf_op jit(solution)/shard_map/all_to_all | solution.py:272
  76.7 0.0 collective-permute-done.1
  76.7 0.0 copy-start.10
  76.7 1.3 dynamic-slice_add_fusion
  78.0 0.0 copy-start.6
  78.0 3.2 %collective-permute-start.3 = (bf16[2,576,128]{2,1,0:T(8,128)(2,1)S(1)}, bf16[2,576,128]{2,1,0:T(8,128)(2,1)S(1)}, u32[]{:S(2)}, u32[]{:S(2)}) collective-permute-start(bf16[2,576,128]{2,1,0:T(8,128)(2,1)S(1)} %get-tuple-element.48), channel_id=1, source_target_pairs={{0,2},{2,0},{1,3},{3,1},{4,6},{6,4},{5,7},{7,5},{8,10},{10,8},{9,1... | collective-permute-start | bytes 884744 | tf_op jit(solution)/shard_map/ppermute | solution.py:279
  81.2 1.6 %all-to-all-done.2 = bf16[32,16,128]{2,1,0:T(8,128)(2,1)S(1)} async-done(((bf16[32,16,128]{2,1,0:T(8,128)(2,1)}), bf16[32,16,128]{2,1,0:T(8,128)(2,1)S(1)}, u32[]{:S(2)}, u32[]{:S(2)}) %all-to-all-start.2) | async-done | bytes 131104 | tf_op jit(solution)/shard_map/all_to_all | solution.py:272
  82.8 13.1 %collective-permute-start.2 = (bf16[16,128]{1,0:T(8,128)(2,1)S(1)}, bf16[16,128]{1,0:T(8,128)(2,1)S(1)}, u32[]{:S(2)}, u32[]{:S(2)}) collective-permute-start(bf16[16,128]{1,0:T(8,128)(2,1)S(1)} %reduce_sum.25), channel_id=1, source_target_pairs={{0,16},{16,0},{1,17},{17,1},{2,18},{18,2},{3,19},{19,3},{4,20},{20... | collective-permute-start | bytes 12296 | tf_op jit(solution)/shard_map/ppermute | solution.py:282
  95.9 2.8 %collective-permute-done.2 = bf16[16,128]{1,0:T(8,128)(2,1)S(1)} collective-permute-done((bf16[16,128]{1,0:T(8,128)(2,1)S(1)}, bf16[16,128]{1,0:T(8,128)(2,1)S(1)}, u32[]{:S(2)}, u32[]{:S(2)}) %collective-permute-start.2) | collective-permute-done | bytes 4128 | tf_op jit(solution)/shard_map/ppermute | solution.py:282
  98.7 0.0 collective-permute-done.3
  98.7 0.1 fusion
  98.8 5.2 %collective-permute-start.4 = (bf16[576,128]{1,0:T(8,128)(2,1)S(1)}, bf16[576,128]{1,0:T(8,128)(2,1)S(1)}, u32[]{:S(2)}, u32[]{:S(2)}) collective-permute-start(bf16[576,128]{1,0:T(8,128)(2,1)S(1)} %get-tuple-element.38), channel_id=1, source_target_pairs={{0,4},{4,0},{1,5},{5,1},{2,6},{6,2},{3,7},{7,3},{8,12},{12,8},{9,1... | collective-permute-start | bytes 442376 | tf_op jit(solution)/shard_map/ppermute | solution.py:293
  104.0 12.0 %all_to_all.25.got_ref = bf16[32,16,128]{2,1,0:T(8,128)(2,1)S(1)} all-to-all(bf16[32,16,128]{2,1,0:T(8,128)(2,1)S(1)} %broadcast_in_dim.10), channel_id=1, replica_groups=mesh['y'=4,'x'=4,'zh'=2,'core'=2,'t2'=2,'t1'=2,'t0'=2] {'y','x','core'}, dimensions={0} | all-to-all | bytes 262144 | tf_op jit(solution)/shard_map/all_to_all | solution.py:294
  115.9 0.0 copy-done.5
  115.9 1.3 rank.1
  117.2 0.0 collective-permute-done.4.came_ref
  117.2 6.3 %all-to-all-start.4 = ((bf16[8,144,128]{2,1,0:T(8,128)(2,1)}), bf16[8,144,128]{2,1,0:T(8,128)(2,1)S(1)}, u32[]{:S(2)}, u32[]{:S(2)}) async-start(bf16[8,144,128]{2,1,0:T(8,128)(2,1)} %get-tuple-element.39), calls=%async_computation.4 | async-start | bytes 589824 | tf_op jit(solution)/shard_map/all_to_all | solution.py:298
  123.6 0.0 copy-done.10
  123.6 0.1 add_convert_fusion.1
  123.7 0.1 convert_element_type.39
  123.8 0.3 fusion.2
  124.1 0.1 pad_maximum_fusion
  124.2 17.4 %all-to-all-done.4.got_ref = bf16[8,144,128]{2,1,0:T(8,128)(2,1)S(1)} async-done(((bf16[8,144,128]{2,1,0:T(8,128)(2,1)}), bf16[8,144,128]{2,1,0:T(8,128)(2,1)S(1)}, u32[]{:S(2)}, u32[]{:S(2)}) %all-to-all-start.4) | async-done | bytes 294944 | tf_op jit(solution)/shard_map/all_to_all | solution.py:298
  141.6 0.0 copy-done.6
  141.6 1.4 finish.1
  (4 shorter events, 0.1 us)
Async XLA Ops:
  0.6 10.5 %copy-start.9 = (bf16[256,4,512]{2,1,0:T(4,128)(2,1)S(1)}, bf16[256,4,512]{2,1,0:T(4,128)(2,1)}, u32[]{:S(2)}) copy-start(bf16[256,4,512]{2,1,0:T(4,128)(2,1)} %param.13) | copy-start | bytes 3145732
  5.1 6.3 %copy-start.3 = (f32[512,64]{0,1:T(8,128)S(1)}, f32[512,64]{0,1:T(8,128)}, u32[]{:S(2)}) copy-start(f32[512,64]{0,1:T(8,128)} %param.10) | copy-start | bytes 393220
  5.1 20.6 %all-to-all-start = ((bf16[4,128,512]{2,1,0:T(8,128)(2,1)}), bf16[4,128,512]{2,1,0:T(8,128)(2,1)}, u32[]{:S(2)}, u32[]{:S(2)}) async-start(bf16[4,128,512]{2,1,0:T(8,128)(2,1)} %partials.1), calls=%async_computation | async-start | bytes 1048576 | tf_op jit(solution)/shard_map/all_to_all | solution.py:261
  11.4 1.0 copy-start.8
  12.5 54.2 %copy-start = (bf16[2048,512]{1,0:T(8,128)(2,1)S(1)}, bf16[2048,512]{1,0:T(8,128)(2,1)}, u32[]{:S(2)}) copy-start(bf16[2048,512]{1,0:T(8,128)(2,1)} %x_ref.3) | copy-start | bytes 6291460
  12.5 54.2 %copy-start.1 = (bf16[2048,64]{0,1:T(8,128)(2,1)S(1)}, bf16[2048,64]{0,1:T(8,128)(2,1)}, u32[]{:S(2)}) copy-start(bf16[2048,64]{0,1:T(8,128)(2,1)} %param.9) | copy-start | bytes 786436
  15.2 0.8 copy-start.2
  16.0 0.8 copy-start.7
  27.5 18.1 %collective-permute-start = (bf16[128,512]{1,0:T(8,128)(2,1)}, bf16[128,512]{1,0:T(8,128)(2,1)S(1)}, u32[]{:S(2)}, u32[]{:S(2)}) collective-permute-start(bf16[128,512]{1,0:T(8,128)(2,1)} %reduce_sum.24), channel_id=1, source_target_pairs={{0,4},{4,0},{1,5},{5,1},{2,6},{6,2},{3,7},{7,3},{8,12},{12,8},{9,1... | collective-permute-start | bytes 393224 | tf_op jit(solution)/shard_map/ppermute | solution.py:265
  47.4 19.3 %all-to-all-start.1 = ((bf16[4,128,512]{2,1,0:T(8,128)(2,1)}), bf16[4,128,512]{2,1,0:T(8,128)(2,1)}, u32[]{:S(2)}, u32[]{:S(2)}) async-start(bf16[4,128,512]{2,1,0:T(8,128)(2,1)} %broadcast_in_dim.4), calls=%async_computation.1 | async-start | bytes 1048576 | tf_op jit(solution)/shard_map/all_to_all | solution.py:268
  51.6 25.1 %collective-permute-start.1 = (bf16[4,576,128]{2,1,0:T(8,128)(2,1)}, bf16[4,576,128]{2,1,0:T(8,128)(2,1)}, u32[]{:S(2)}, u32[]{:S(2)}) collective-permute-start(bf16[4,576,128]{2,1,0:T(8,128)(2,1)} %copy-done.7), channel_id=1, source_target_pairs={{0,1},{1,0},{2,3},{3,2},{4,5},{5,4},{6,7},{7,6},{8,9},{9,8},{10,11... | collective-permute-start | bytes 1769480 | tf_op jit(solution)/shard_map/ppermute | solution.py:271
  68.3 0.7 copy-start.4
  69.0 47.0 %copy-start.5 = (f32[64,64]{1,0:T(8,128)S(1)}, f32[64,64]{1,0:T(8,128)}, u32[]{:S(2)}) copy-start(f32[64,64]{1,0:T(8,128)} %b_ref.5) | copy-start | bytes 49156
  69.0 13.8 %all-to-all-start.2 = ((bf16[32,16,128]{2,1,0:T(8,128)(2,1)}), bf16[32,16,128]{2,1,0:T(8,128)(2,1)S(1)}, u32[]{:S(2)}, u32[]{:S(2)}) async-start(bf16[32,16,128]{2,1,0:T(8,128)(2,1)} %copy-done.4), calls=%async_computation.2 | async-start | bytes 262144 | tf_op jit(solution)/shard_map/all_to_all | solution.py:272
  76.7 46.9 %copy-start.10 = (s32[32]{0:T(128)S(1)}, s32[32]{0:T(128)}, u32[]{:S(2)}) copy-start(s32[32]{0:T(128)} %param.14) | copy-start | bytes 388
  78.0 63.6 %copy-start.6 = (f32[128]{0:T(128)S(1)}, f32[128]{0:T(128)}, u32[]{:S(2)}) copy-start(f32[128]{0:T(128)} %param.15) | copy-start | bytes 1540
  78.0 20.7 %collective-permute-start.3 = (bf16[2,576,128]{2,1,0:T(8,128)(2,1)S(1)}, bf16[2,576,128]{2,1,0:T(8,128)(2,1)S(1)}, u32[]{:S(2)}, u32[]{:S(2)}) collective-permute-start(bf16[2,576,128]{2,1,0:T(8,128)(2,1)S(1)} %get-tuple-element.48), channel_id=1, source_target_pairs={{0,2},{2,0},{1,3},{3,1},{4,6},{6,4},{5,7},{7,5},{8,10},{10,8},{9,1... | collective-permute-start | bytes 884744 | tf_op jit(solution)/shard_map/ppermute | solution.py:279
  82.8 15.9 %collective-permute-start.2 = (bf16[16,128]{1,0:T(8,128)(2,1)S(1)}, bf16[16,128]{1,0:T(8,128)(2,1)S(1)}, u32[]{:S(2)}, u32[]{:S(2)}) collective-permute-start(bf16[16,128]{1,0:T(8,128)(2,1)S(1)} %reduce_sum.25), channel_id=1, source_target_pairs={{0,16},{16,0},{1,17},{17,1},{2,18},{18,2},{3,19},{19,3},{4,20},{20... | collective-permute-start | bytes 12296 | tf_op jit(solution)/shard_map/ppermute | solution.py:282
  98.8 18.5 %collective-permute-start.4 = (bf16[576,128]{1,0:T(8,128)(2,1)S(1)}, bf16[576,128]{1,0:T(8,128)(2,1)S(1)}, u32[]{:S(2)}, u32[]{:S(2)}) collective-permute-start(bf16[576,128]{1,0:T(8,128)(2,1)S(1)} %get-tuple-element.38), channel_id=1, source_target_pairs={{0,4},{4,0},{1,5},{5,1},{2,6},{6,2},{3,7},{7,3},{8,12},{12,8},{9,1... | collective-permute-start | bytes 442376 | tf_op jit(solution)/shard_map/ppermute | solution.py:293
  117.2 24.4 %all-to-all-start.4 = ((bf16[8,144,128]{2,1,0:T(8,128)(2,1)}), bf16[8,144,128]{2,1,0:T(8,128)(2,1)S(1)}, u32[]{:S(2)}, u32[]{:S(2)}) async-start(bf16[8,144,128]{2,1,0:T(8,128)(2,1)} %get-tuple-element.39), calls=%async_computation.4 | async-start | bytes 589824 | tf_op jit(solution)/shard_map/all_to_all | solution.py:298
